TPU v7x, 32 devices: a whole 2x2x4 slice. The times are simulated.
32 devices in a mesh: lat: 8 (over z, core), freq: 4 (over y, x).
Axes of the slice: x: 2, y: 2, z: 4, core: 2. Of those that a mesh axis runs over, the one named last changes fastest.
Arguments:
- wavefield: float32 [2, 8, 2048, 2048], P(None, 'freq', 'lat'), may hold values from -6 to 6
- source_field: float32 [2, 8, 2048, 2048], P(None, 'freq', 'lat'), may hold values from -6 to 6
- slowness: float32 [2048, 2048], P('lat', 'freq'), may hold values from 0.00015 to 0.00094
- freq_index: int32 [8], P('freq'), may hold values from 192 to 767, as said below
Outputs:
- next_field: float32 [2, 8, 2048, 2048], P(None, 'freq', 'lat')
- image: float32 [2048, 2048], P('lat', 'freq')
Inputs may be any that keep to these rules, and one draw needn't show every extreme that they name: `freq_index`: distinct frequency indices.
All inputs are finite; a program needn't handle non-finite values.
Results may differ from a plain program's by a relative error of at most 0.00013.
Values sent between devices are 32-bit elements; how exact they have to be, the bound alone decides.
A program may use at most 128 MiB of HBM per device.

v0:
```python
import math

import jax
import jax.numpy as jnp
from jax import lax
from jax.sharding import PartitionSpec as P

NX = 2048
NY = 2048


depth_step = 10.0
grid_step = 25.0
freq_step = 0.0625
highest = lax.Precision.HIGHEST
first_factor = 32


def extended(cells, sides, width):
    for axis, dim in sides:
        count = lax.axis_size(axis)
        ends = count - 1
        head = lax.slice_in_dim(cells, 0, width, axis=dim)
        tail = lax.slice_in_dim(cells, cells.shape[dim] - width, cells.shape[dim], axis=dim)
        cells = jnp.concatenate(
            [
                lax.ppermute(tail, axis, [(i, (i + 1) % count) for i in range(ends)]),
                cells,
                lax.ppermute(head, axis, [((i + 1) % count, i) for i in range(ends)]),
            ],
            axis=dim,
        )
    return cells


def fourier_tables(count):
    indices = lax.iota(jnp.int32, count)
    product = indices[:, None] * indices[None, :] % count
    angles = 2.0 * math.pi / count * product.astype(jnp.float32)
    return (jnp.cos(angles), jnp.sin(angles))


def twiddle_tables(outer, inner, count):
    left = lax.iota(jnp.int32, outer)
    right = lax.iota(jnp.int32, inner)
    product = left[:, None] * right[None, :] % count
    angles = 2.0 * math.pi / count * product.astype(jnp.float32)
    return (jnp.cos(angles), jnp.sin(angles))


def signed_waves(indices, count):
    signed = jnp.where(indices < count // 2, indices, indices - count)
    return 2.0 * math.pi / (count * grid_step) * signed.astype(jnp.float32)


def table_product(form, cos_t, sin_t, real, imag, sign):
    new_real = jnp.einsum(form, cos_t, real, precision=highest) - sign * jnp.einsum(
        form, sin_t, imag, precision=highest
    )
    new_imag = jnp.einsum(form, cos_t, imag, precision=highest) + sign * jnp.einsum(
        form, sin_t, real, precision=highest
    )
    return (new_real, new_imag)


def transform_axis(real, imag, sign, middle):
    if middle:
        members, count, other = real.shape
    else:
        members, other, count = real.shape
    inner = count // first_factor
    cos_a, sin_a = fourier_tables(first_factor)
    cos_b, sin_b = fourier_tables(inner)
    tw_cos, tw_sin = twiddle_tables(first_factor, inner, count)
    if middle:
        real = real.reshape(members, first_factor, inner, other)
        imag = imag.reshape(members, first_factor, inner, other)
        real, imag = table_product("ka,fabc->fkbc", cos_a, sin_a, real, imag, sign)
        tw_cos = tw_cos[None, :, :, None]
        tw_sin = tw_sin[None, :, :, None]
        form_two = "lb,fkbc->flkc"
    else:
        real = real.reshape(members, other, first_factor, inner)
        imag = imag.reshape(members, other, first_factor, inner)
        real, imag = table_product("ka,frab->frkb", cos_a, sin_a, real, imag, sign)
        tw_cos = tw_cos[None, None]
        tw_sin = tw_sin[None, None]
        form_two = "lb,frkb->frlk"
    turned_real = real * tw_cos - sign * imag * tw_sin
    turned_imag = imag * tw_cos + sign * real * tw_sin
    real, imag = table_product(form_two, cos_b, sin_b, turned_real, turned_imag, sign)
    if middle:
        return (real.reshape(members, count, other), imag.reshape(members, count, other))
    return (real.reshape(members, other, count), imag.reshape(members, other, count))


def spectral_step(real_part, imag_part, angular, mean_slow):
    total_y = real_part.shape[2]
    fwd_real, fwd_imag = transform_axis(real_part, imag_part, -1.0, False)
    columns = lax.all_to_all(
        jnp.stack([fwd_real, fwd_imag]), "lat", split_axis=3, concat_axis=2, tiled=True
    )
    total_x = columns.shape[2]
    spec_real, spec_imag = transform_axis(columns[0], columns[1], -1.0, True)
    width = columns.shape[3]
    col_index = lax.axis_index("lat") * width + lax.iota(jnp.int32, width)
    wave_y = signed_waves(col_index, total_y)
    wave_x = signed_waves(lax.iota(jnp.int32, total_x), total_x)
    vertical = (
        (angular * mean_slow)[:, None, None] ** 2
        - wave_x[None, :, None] ** 2
        - wave_y[None, None, :] ** 2
    )
    damping = jnp.exp(-jnp.sqrt(jnp.maximum(-vertical, 0.0)) * depth_step)
    advance = jnp.sqrt(jnp.maximum(vertical, 0.0)) * depth_step
    turn_real = damping * jnp.cos(advance)
    turn_imag = damping * jnp.sin(advance)
    shift_real = spec_real * turn_real - spec_imag * turn_imag
    shift_imag = spec_real * turn_imag + spec_imag * turn_real
    back_real, back_imag = transform_axis(shift_real, shift_imag, 1.0, True)
    back_real = back_real / total_x
    back_imag = back_imag / total_x
    strips = lax.all_to_all(
        jnp.stack([back_real, back_imag]), "lat", split_axis=2, concat_axis=3, tiled=True
    )
    out_real, out_imag = transform_axis(strips[0], strips[1], 1.0, False)
    return (out_real / total_y, out_imag / total_y)


def local(wavefield, source_field, slowness, freq_index):
    members = wavefield.shape[1]
    strip = lax.all_gather(slowness, "freq", axis=1, tiled=True)
    total = lax.psum(jnp.sum(strip), "lat")
    mean_slow = total / (NX * NY)
    angular = 2.0 * math.pi * freq_step * freq_index.astype(jnp.float32)
    lens_angle = angular[:, None, None] * (strip - mean_slow)[None] * depth_step
    lens_cos = jnp.cos(lens_angle)
    lens_sin = jnp.sin(lens_angle)
    real_part = wavefield[0] * lens_cos - wavefield[1] * lens_sin
    imag_part = wavefield[0] * lens_sin + wavefield[1] * lens_cos
    prop_real, prop_imag = spectral_step(real_part, imag_part, angular, mean_slow)
    stacked = jnp.stack([prop_real, prop_imag])
    padded = extended(stacked, (("lat", 2),), 1)
    side_pad = jnp.pad(stacked, ((0, 0), (0, 0), (0, 0), (1, 1)))
    beside_all = (
        padded[:, :, 2:, :] + padded[:, :, :-2, :] + side_pad[:, :, :, 2:] + side_pad[:, :, :, :-2]
    )
    laplace = beside_all - 4.0 * stacked
    lateral_gain = (
        depth_step
        * (
            0.5 / (angular[:, None, None] * mean_slow)
            - 0.5 / (angular[:, None, None] * strip[None])
        )
        / (grid_step * grid_step)
    )
    new_real = prop_real + lateral_gain * laplace[1]
    new_imag = prop_imag - lateral_gain * laplace[0]
    batch_total = members * lax.axis_size("freq")
    terms = jnp.sum(new_real * source_field[0] + new_imag * source_field[1], axis=0) / math.sqrt(
        batch_total
    )
    image = lax.psum_scatter(terms, "freq", scatter_dimension=1, tiled=True)
    return (jnp.stack([new_real, new_imag]), image)


def solution(mesh):
    return jax.shard_map(
        local,
        mesh=mesh,
        in_specs=(
            P(None, "freq", "lat", None),
            P(None, "freq", "lat", None),
            P("lat", "freq"),
            P("freq"),
        ),
        out_specs=(P(None, "freq", "lat", None), P("lat", "freq")),
        check_vma=False,
    )
```

profile of v0, /device:TPU:0, one launch (start us, length us, event | category | flops | bytes accessed | tf_op | source)
XLA Modules:
  0.0 928.1 jit_solution(8928447778791640208)
XLA Ops:
  9.3 8.0 fusion.360
  22.8 25.7 %all-gather.2.cloned.1.call-done = f32[256,2048]{0,1:T(8,128)} async-done(((f32[256,512]{0,1:T(8,128)}), f32[256,2048]{0,1:T(8,128)}) %all-gather.2.cloned.1.call-update) | async-done | bytes 2097168 | tf_op jit(solution)/shard_map/all_gather | solution.py:132
  56.7 17.0 %psum.7 = f32[]{:T(128)} all-reduce(f32[]{:T(128)} %reduce_sum.18), channel_id=1, replica_groups=mesh['lat'=8,'freq'=4] {'lat'}, use_global_device_ids=true, to_apply=%region_1.0 | all-reduce | flops 1 | bytes 8 | tf_op jit(solution)/shard_map/psum | solution.py:133
  77.2 17.5 %multiply_subtract_fusion.3 = (f32[2,256,32,64]{1,3,2,0:T(8,128)S(1)}, f32[2,256,32,64]{1,3,2,0:T(8,128)S(1)}) fusion(f32[2,256,32,64]{1,3,2,0:T(8,128)} %bitcast.236, f32[2,256,32,64]{1,3,2,0:T(8,128)S(1)} %bitcast.235, f32[256,32,64]{0,2,1:T(8,128)S(1)} %bitcast.243, f32[2]{0:T(128)S(1)} %get-tuple-element.34), kind=kLoop, calls=%fused_computation.85 | loop fusion | flops 8388608 | bytes 18874376 | tf_op jit(solution)/shard_map/sub | solution.py:139
  115.4 8.3 fusion.29
  156.9 16.5 %copy.145 = f32[2,2,256,2048]{2,1,0,3:T(2,128)} copy(f32[2,2,256,2048]{2,3,1,0:T(8,128)S(1)} %pad_maximum_fusion.5) | data formatting | bytes 16777216 | tf_op jit(solution)/shard_map/stack | solution.py:101
  179.0 183.6 %all-to-all-done = f32[2,2,256,2048]{2,1,0,3:T(2,128)} async-done(((f32[2,2,256,2048]{2,1,0,3:T(2,128)}), f32[2,2,256,2048]{2,1,0,3:T(2,128)}, u32[]{:S(2)}, u32[]{:S(2)}) %all-to-all-start) | async-done | bytes 8388640 | tf_op jit(solution)/shard_map/all_to_all | solution.py:100
  377.0 10.4 %fusion.75 = f32[2,64,256,32]{2,3,1,0:T(8,128)} fusion(f32[2,32,64,256]{3,2,1,0:T(8,128)} %bitcast.229), kind=kOutput, calls=%fused_computation.131 | convolution fusion | flops 402667520 | bytes 8388608 | tf_op jit(solution)/shard_map/ka,fabc->fkbc/dot_general | solution.py:57
  400.1 10.3 %multiply_subtract_fusion.1 = f32[2,64,256,32]{2,3,1,0:T(8,128)S(1)} fusion(f32[2,64,256,32]{2,3,1,0:T(8,128)} %fusion.75, f32[2,32,64,256]{3,2,1,0:T(8,128)} %bitcast.227), kind=kOutput, calls=%fused_computation.79 | convolution fusion | flops 404764672 | bytes 12582912 | tf_op jit(solution)/shard_map/ka,fabc->fkbc/dot_general | solution.py:57
  410.4 8.4 fusion.27
  451.4 19.5 %fusion.25 = (f32[2,32,64,256]{3,2,1,0:T(8,128)S(1)}, f32[2,32,64,256]{3,2,1,0:T(8,128)S(1)}) fusion(f32[256]{0:T(256)S(1)} %fusion.226, f32[2,32,64]{2,1,0:T(8,128)S(1)} %broadcast_subtract_fusion.1, f32[2,32,64,256]{3,2,1,0:T(8,128)S(1)} %bitcast.239, f32[2,32,64,256]{3,2,1,0:T(8,128)S(1)} %bitcast.237), kind=kLoop, calls=%fused_computation.53 | loop fusion | flops 15728640 | bytes 16794624 | tf_op jit(solution)/shard_map/sub | solution.py:118
  491.4 8.4 fusion.23
  532.9 16.7 %copy.169 = f32[2,2,2048,256]{3,1,0,2:T(2,128)} copy(f32[2,2,2048,256]{3,2,1,0:T(8,128)S(1)} %pad_maximum_fusion.6) | data formatting | bytes 16777216 | tf_op jit(solution)/shard_map/stack | solution.py:124
  554.6 7.8 fusion.357
  573.2 165.3 %all-to-all-done.1 = f32[2,2,2048,256]{3,1,0,2:T(2,128)} async-done(((f32[2,2,2048,256]{3,1,0,2:T(2,128)}), f32[2,2,2048,256]{3,1,0,2:T(2,128)}, u32[]{:S(2)}, u32[]{:S(2)}) %all-to-all-start.1) | async-done | bytes 8388640 | tf_op jit(solution)/shard_map/all_to_all | solution.py:123
  752.8 10.4 %fusion.43 = f32[2,256,64,32]{1,3,2,0:T(8,128)} fusion(f32[2,256,32,64]{1,3,2,0:T(8,128)} %bitcast.231), kind=kOutput, calls=%fused_computation.99 | convolution fusion | flops 402667520 | bytes 8388608 | tf_op jit(solution)/shard_map/ka,frab->frkb/dot_general | solution.py:57
  763.3 7.5 fusion.41
  776.1 10.4 %fusion.103 = f32[2,256,64,32]{1,3,2,0:T(8,128)S(1)} fusion(f32[2,256,64,32]{1,3,2,0:T(8,128)} %fusion.43, f32[2,256,32,64]{1,3,2,0:T(8,128)} %bitcast.225), kind=kOutput, calls=%fused_computation.155 | convolution fusion | flops 403716096 | bytes 12582912 | tf_op jit(solution)/shard_map/ka,frab->frkb/dot_general | solution.py:57
  786.5 8.4 fusion.21
  817.8 7.3 multiply_bitcast_fusion.1
  842.2 7.4 pad_maximum_fusion
  855.1 21.9 %fusion.3 = f32[2,2,256,2048]{2,3,1,0:T(8,128)} fusion(f32[2,2,1,2048]{2,3,1,0:T(8,128)} %copy.186, f32[1,2,256,2048]{2,3,1,0:T(8,128)} %bitcast.221, f32[1,2,256,2048]{2,3,1,0:T(8,128)} %bitcast.224, f32[2,2,1,2048]{2,3,1,0:T(8,128)} %copy.184, f32[2,2,256,2048]{2,3,1,0:T(8,128)} %pad_maximum_fusion), kind=kLoop, calls=%fused_computation.9 | loop fusion | flops 18874368 | bytes 25231360 | tf_op jit(solution)/shard_map/sub | solution.py:148
  896.7 8.7 copy.191
  905.4 13.6 %reduce-scatter.2.cloned.1.call-done = f32[256,512]{0,1:T(8,128)} async-done(((f32[256,2048]{0,1:T(8,128)}), f32[256,512]{0,1:T(8,128)}) %reduce-scatter.2.cloned.1.call-update) | async-done | bytes 524304 | tf_op jit(solution)/shard_map/reduce_scatter | solution.py:163
  (107 shorter events, 293.0 us)
Async XLA Ops:
  7.2 41.3 %all-gather.2.cloned.1.call-start = ((), (), s32[]{:S(2)}) async-start(), calls=%async_computation.3 | async-start | bytes 2621440 | tf_op jit(solution)/shard_map/all_gather | solution.py:132
  51.2 23.8 %copy-start.16 = (s32[2]{0:T(128)S(1)}, s32[2]{0:T(128)}, u32[]{:S(2)}) copy-start(s32[2]{0:T(128)} %param.7) | copy-start | bytes 28
  51.2 24.3 %copy-start.8 = (f32[256,2048]{0,1:T(8,128)S(1)}, f32[256,2048]{0,1:T(8,128)}, u32[]{:S(2)}) copy-start(f32[256,2048]{0,1:T(8,128)} %all-gather.2.cloned.1.call-done) | copy-start | bytes 6291460
  75.0 2.2 copy-start.12
  75.5 19.2 %copy-start.13 = (f32[2]{0:T(128)}, f32[2]{0:T(128)S(1)}, u32[]{:S(2)}) copy-start(f32[2]{0:T(128)S(1)} %get-tuple-element.34) | copy-start | bytes 28
  173.4 189.3 %all-to-all-start = ((f32[2,2,256,2048]{2,1,0,3:T(2,128)}), f32[2,2,256,2048]{2,1,0,3:T(2,128)}, u32[]{:S(2)}, u32[]{:S(2)}) async-start(f32[2,2,256,2048]{2,1,0,3:T(2,128)} %copy.145), calls=%async_computation | async-start | bytes 16777216 | tf_op jit(solution)/shard_map/all_to_all | solution.py:100
  377.0 10.4 %copy-start.6 = (f32[1,2,8,256,256]{4,3,2,1,0:T(8,128)S(1)}, f32[1,2,8,256,256]{4,3,2,1,0:T(8,128)}, u32[]{:S(2)}) copy-start(f32[1,2,8,256,256]{4,3,2,1,0:T(8,128)} %copy.149) | copy-start | bytes 12582916
  400.0 10.4 %copy-start.5 = (f32[1,2,8,256,256]{4,3,2,1,0:T(8,128)S(1)}, f32[1,2,8,256,256]{4,3,2,1,0:T(8,128)}, u32[]{:S(2)}) copy-start(f32[1,2,8,256,256]{4,3,2,1,0:T(8,128)} %copy.147) | copy-start | bytes 12582916
  400.0 10.4 %copy-start.11 = (f32[2,64,256,32]{2,3,1,0:T(8,128)S(1)}, f32[2,64,256,32]{2,3,1,0:T(8,128)}, u32[]{:S(2)}) copy-start(f32[2,64,256,32]{2,3,1,0:T(8,128)} %fusion.73) | copy-start | bytes 12582916
  549.6 188.9 %all-to-all-start.1 = ((f32[2,2,2048,256]{3,1,0,2:T(2,128)}), f32[2,2,2048,256]{3,1,0,2:T(2,128)}, u32[]{:S(2)}, u32[]{:S(2)}) async-start(f32[2,2,2048,256]{3,1,0,2:T(2,128)} %copy.169), calls=%async_computation.1 | async-start | bytes 16777216 | tf_op jit(solution)/shard_map/all_to_all | solution.py:123
  554.6 364.5 %reduce-scatter.2.cloned.1.call-start = ((), (), s32[]{:S(2)}) async-start(), calls=%async_computation.4 | async-start | bytes 2621440 | tf_op jit(solution)/shard_map/reduce_scatter | solution.py:163
  752.8 10.5 %copy-start.7 = (f32[1,2,256,8,256]{2,4,3,1,0:T(8,128)S(1)}, f32[1,2,256,8,256]{2,4,3,1,0:T(8,128)}, u32[]{:S(2)}) copy-start(f32[1,2,256,8,256]{2,4,3,1,0:T(8,128)} %copy.173) | copy-start | bytes 12582916
  776.1 10.4 %copy-start.4 = (f32[1,2,256,8,256]{2,4,3,1,0:T(8,128)S(1)}, f32[1,2,256,8,256]{2,4,3,1,0:T(8,128)}, u32[]{:S(2)}) copy-start(f32[1,2,256,8,256]{2,4,3,1,0:T(8,128)} %copy.171) | copy-start | bytes 12582916
  776.1 10.4 %copy-start.10 = (f32[2,256,64,32]{1,3,2,0:T(8,128)S(1)}, f32[2,256,64,32]{1,3,2,0:T(8,128)}, u32[]{:S(2)}) copy-start(f32[2,256,64,32]{1,3,2,0:T(8,128)} %fusion.41) | copy-start | bytes 12582916
  817.8 9.8 %copy-start = (f32[2,256,64,32]{1,3,2,0:T(8,128)}, f32[2,256,64,32]{1,3,2,0:T(8,128)S(1)}, u32[]{:S(2)}) copy-start(f32[2,256,64,32]{1,3,2,0:T(8,128)S(1)} %copy.182) | copy-start | bytes 12582916
  827.6 4.6 copy-start.2
  835.0 14.6 %collective-permute-start = (f32[2,2,1,2048]{3,1,2,0:T(2,128)S(1)}, f32[2,2,1,2048]{3,1,2,0:T(2,128)S(1)}, u32[]{:S(2)}, u32[]{:S(2)}) collective-permute-start(f32[2,2,1,2048]{3,1,2,0:T(2,128)S(1)} %copy.183), channel_id=1, source_target_pairs={{4,0},{8,4},{12,8},{16,12},{20,16},{24,20},{28,24},{5,1},{9,5},{13... | collective-permute-start | bytes 98312 | tf_op jit(solution)/shard_map/ppermute | solution.py:29
  839.2 13.2 %collective-permute-start.1 = (f32[2,2,1,2048]{3,1,2,0:T(2,128)S(1)}, f32[2,2,1,2048]{3,1,2,0:T(2,128)S(1)}, u32[]{:S(2)}, u32[]{:S(2)}) collective-permute-start(f32[2,2,1,2048]{3,1,2,0:T(2,128)S(1)} %copy.185), channel_id=1, source_target_pairs={{0,4},{4,8},{8,12},{12,16},{16,20},{20,24},{24,28},{1,5},{5,9},{9,... | collective-permute-start | bytes 98312 | tf_op jit(solution)/shard_map/ppermute | solution.py:27
  855.0 21.9 %copy-start.1 = (f32[2,256,64,32]{1,3,2,0:T(8,128)S(1)}, f32[2,256,64,32]{1,3,2,0:T(8,128)}, u32[]{:S(2)}) copy-start(f32[2,256,64,32]{1,3,2,0:T(8,128)} %copy-done) | copy-start | bytes 12582916
  855.1 21.9 %copy-start.3 = (f32[2,256,64,32]{1,3,2,0:T(8,128)S(1)}, f32[2,256,64,32]{1,3,2,0:T(8,128)}, u32[]{:S(2)}) copy-start(f32[2,256,64,32]{1,3,2,0:T(8,128)} %copy-done.2) | copy-start | bytes 12582916
  855.1 21.9 %copy-start.9 = (f32[256,2048]{0,1:T(8,128)S(1)}, f32[256,2048]{0,1:T(8,128)}, u32[]{:S(2)}) copy-start(f32[256,2048]{0,1:T(8,128)} %all-gather.2.cloned.1.call-done) | copy-start | bytes 6291460
  855.1 21.9 %copy-start.14 = (f32[2]{0:T(128)S(1)}, f32[2]{0:T(128)}, u32[]{:S(2)}) copy-start(f32[2]{0:T(128)} %copy-done.13) | copy-start | bytes 28
  855.1 21.9 %copy-start.15 = (f32[2]{0:T(128)S(1)}, f32[2]{0:T(128)}, u32[]{:S(2)}) copy-start(f32[2]{0:T(128)} %get-tuple-element.32) | copy-start | bytes 28
Sparse Core Ops, SparseCore 0:
  10.4 38.0 all-gather.1
  885.9 33.0 reduce-scatter.1
where the time goes:
time: 933 us; the launch traced here: 928 us
  waiting for transfers between devices  388 us (42%)
  matrix products  241 us (26%)
  local copies, waits for them, and re-layouts  156 us (17%)
  other arithmetic  95.3 us (10%)
  blocking collectives  17 us (2%)
  between operations  16.1 us (2%)
  starting transfers between devices  14.7 us (2%)
    all_to_all x1, waiting for transfers between devices, spectral_step(): lax.all_to_all(jnp.stack([fwd_real, fwd_imag]), 'lat', split_axis=3, conc...  184 us
    all_to_all x1, waiting for transfers between devices, spectral_step(): lax.all_to_all(jnp.stack([back_real, back_imag]), 'lat', split_axis=2, co...  165 us
    dot_general x8, matrix products, table_product(): jnp.einsum(form, cos_t, real, precision=highest)  62.6 us
    dot_general x8, matrix products, table_product(): jnp.einsum(form, sin_t, real, precision=highest)  61.6 us
    dot_general x8, matrix products, table_product(): jnp.einsum(form, sin_t, imag, precision=highest)  60.6 us
    dot_general x8, matrix products, table_product(): jnp.einsum(form, cos_t, imag, precision=highest)  56.2 us
    unnamed x41, local copies, waits for them, and re-layouts  36.1 us
    all_gather x1, waiting for transfers between devices, local(): strip = lax.all_gather(slowness, 'freq', axis=1, tiled=True)  25.7 us
  transfers between devices with their start and end apart: 6, of which 4 were waited for; matrix products, arithmetic and copies ran while one was open for 7% of the time, Pallas kernels for 0%

commit v1 on v0

v1 whole, which is shorter than its diff:
```python
import functools
import math

import jax
import jax.numpy as jnp
import numpy as np
from jax import lax
from jax.experimental import pallas as pl
from jax.experimental.pallas import tpu as pltpu
from jax.sharding import PartitionSpec as P

depth_step = 10.0
grid_step = 25.0
freq_step = 0.0625
LANES = 128
HALO = 8
VMEM_BYTES = 48 * 1024 * 1024


def dft_tables(sign):
    i = np.arange(LANES)
    ang = 2.0 * math.pi / LANES * ((i[:, None] * i[None, :]) % LANES)
    c, s = np.cos(ang), sign * np.sin(ang)
    return np.block([[c, s], [-s, c]])


def split_table(table):
    high = jnp.asarray(table.astype(np.float32)).astype(jnp.bfloat16)
    high64 = np.asarray(table.astype(np.float32).astype(jnp.bfloat16)).astype(np.float64)
    low = (table - high64).astype(np.float32).astype(jnp.bfloat16)
    return jnp.stack([high, jnp.asarray(low)])


def twiddle(count):
    factor = count // LANES
    k, n = np.arange(factor), np.arange(LANES)
    ang = 2.0 * math.pi / count * ((k[:, None] * n[None, :]) % count)
    return np.stack([np.cos(ang), np.sin(ang)]).astype(np.float32)


def fft_list(values, sign):
    count = len(values)
    if count == 1:
        return values
    even, odd = fft_list(values[0::2], sign), fft_list(values[1::2], sign)
    low, high = [], []
    for k in range(count // 2):
        (er, ei), (r, i) = even[k], odd[k]
        if k == 0:
            tr, ti = r, i
        elif 4 * k == count:
            tr, ti = (-i, r) if sign > 0 else (i, -r)
        else:
            c = math.cos(2.0 * math.pi * k / count)
            s = sign * math.sin(2.0 * math.pi * k / count)
            if abs(abs(c) - abs(s)) < 1e-9:
                h = math.sqrt(0.5)
                sc, ss = (1 if c > 0 else -1), (1 if s > 0 else -1)
                tr = h * (r - i) if sc * ss > 0 else h * (r + i)
                ti = h * (i + r) if sc * ss > 0 else h * (i - r)
                if sc < 0:
                    tr, ti = -tr, -ti
            else:
                tr, ti = c * r - s * i, c * i + s * r
        low.append((er + tr, ei + ti))
        high.append((er - tr, ei - ti))
    return low + high


def sin_cos(angle):
    turns = jnp.round(angle * (0.5 / math.pi))
    r = angle - turns * 6.28125 - turns * (2.0 * math.pi - 6.28125)
    r2 = r * r
    s = jnp.full_like(r, 1.0 / math.factorial(17))
    for n in range(15, 0, -2):
        s = s * r2 + ((-1) ** (n // 2)) / math.factorial(n)
    c = jnp.full_like(r, -1.0 / math.factorial(18))
    for n in range(16, -1, -2):
        c = c * r2 + ((-1) ** (n // 2)) / math.factorial(n)
    return s * r, c


def split(x):
    high = x.astype(jnp.bfloat16)
    return high, (x - high.astype(jnp.float32)).astype(jnp.bfloat16)


def dot(a, b):
    return jnp.dot(a, b, preferred_element_type=jnp.float32)


def forward_kernel(ang_ref, wave_ref, slow_ref, tw_ref, m_ref, out_ref, zs, *, member):
    factor, block = zs.shape[0], zs.shape[1]
    part_width, width = slow_ref.shape[2], out_ref.shape[3]
    scale = ang_ref[member] * depth_step

    def tile(t, carry):
        rows = pl.ds(pl.multiple_of(t * 8, 8), 8)
        cells = []
        for n in range(factor):
            at = n * LANES
            s = slow_ref[at // part_width, rows, pl.ds(at % part_width, LANES)]
            sn, cs = sin_cos(s * scale)
            re = wave_ref[0, 0, rows, pl.ds(at, LANES)]
            im = wave_ref[1, 0, rows, pl.ds(at, LANES)]
            cells.append((re * cs - im * sn, re * sn + im * cs))
        for k, (re, im) in enumerate(fft_list(cells, -1.0)):
            if k:
                c, s = tw_ref[0, pl.ds(k, 1), :], tw_ref[1, pl.ds(k, 1), :]
                re, im = re * c + im * s, im * c - re * s
            zs[k, rows, pl.ds(0, LANES)] = re
            zs[k, rows, pl.ds(LANES, LANES)] = im
        return carry

    lax.fori_loop(0, block // 8, tile, 0)
    for g in range(0, factor, 4):
        high, low = split(zs[pl.ds(g, 4)].reshape(4 * block, 2 * LANES))
        y = dot(high, m_ref[0]) + (dot(low, m_ref[0]) + dot(high, m_ref[1]))
        y = y.reshape(4, block, 2 * LANES)
        for j in range(4):
            at = (g + j) * LANES
            cols = pl.ds(at % width, LANES)
            out_ref[at // width, 0, :, cols] = y[j, :, :LANES]
            out_ref[at // width, 1, :, cols] = y[j, :, LANES:]


def shift_kernel(ang_ref, mean_ref, in_ref, tw_ref, m_ref, out_ref, zs, *, member):
    factor, width = zs.shape[0], zs.shape[2]
    strips, rows_in = in_ref.shape[0], in_ref.shape[2]
    count = factor * LANES
    base = lax.axis_index("lat") * width

    def tile_in(t, carry):
        r = pl.multiple_of(t * 8, 8)
        for lane in range(0, width, LANES):
            lanes = pl.ds(lane, LANES)
            cells = []
            for n in range(factor):
                at = n * LANES
                rows = pl.ds(at % rows_in + r, 8)
                cells.append(
                    (in_ref[at // rows_in, 0, rows, lanes], in_ref[at // rows_in, 1, rows, lanes])
                )
            for k, (re, im) in enumerate(fft_list(cells, -1.0)):
                if k:
                    c, s = tw_ref[0, k, pl.ds(r, 8), :], tw_ref[1, k, pl.ds(r, 8), :]
                    re, im = re * c + im * s, im * c - re * s
                zs[k, pl.ds(r, 8), lanes] = re
                zs[k, pl.ds(LANES + r, 8), lanes] = im
        return carry

    lax.fori_loop(0, LANES // 8, tile_in, 0)

    flat = angular_mean = ang_ref[member] * mean_ref[0]
    flat = angular_mean * depth_step
    place = base + lax.broadcasted_iota(jnp.int32, (LANES, width), 1)
    index_y = place // LANES + factor * (place % LANES)
    signed_y = jnp.where(index_y < count // 2, index_y, index_y - count)
    wave_y = 2.0 * math.pi / (count * grid_step) * signed_y.astype(jnp.float32)
    rest = angular_mean * angular_mean - wave_y * wave_y
    row = lax.broadcasted_iota(jnp.int32, (LANES, width), 0)

    def product(k, carry):
        high, low = split(zs[k])
        y = dot(m_ref[0], high) + (dot(m_ref[0], low) + dot(m_ref[1], high))
        index_x = k + factor * row
        signed_x = jnp.where(index_x < count // 2, index_x, index_x - count)
        wave_x = 2.0 * math.pi / (count * grid_step) * signed_x.astype(jnp.float32)
        vertical = rest - wave_x * wave_x
        size = jnp.sqrt(jnp.abs(vertical)) * depth_step
        damping = jnp.where(vertical < 0.0, jnp.exp(-size), 1.0) * (1.0 / (count * count))
        sn, cs = sin_cos(jnp.where(vertical > 0.0, size, 0.0) - flat)
        tr, ti = damping * cs, damping * sn
        re, im = y[:LANES], y[LANES:]
        z = jnp.concatenate([re * tr - im * ti, re * ti + im * tr], axis=0)
        high, low = split(z)
        zs[k] = dot(m_ref[2], high) + (dot(m_ref[2], low) + dot(m_ref[3], high))
        return carry

    lax.fori_loop(0, factor, product, 0)

    def tile_out(t, carry):
        r = pl.multiple_of(t * 8, 8)
        for lane in range(0, width, LANES):
            lanes = pl.ds(lane, LANES)
            cells = []
            for k in range(factor):
                re, im = zs[k, pl.ds(r, 8), lanes], zs[k, pl.ds(LANES + r, 8), lanes]
                if k:
                    c, s = tw_ref[0, k, pl.ds(r, 8), :], tw_ref[1, k, pl.ds(r, 8), :]
                    re, im = re * c - im * s, im * c + re * s
                cells.append((re, im))
            for n, (re, im) in enumerate(fft_list(cells, 1.0)):
                at = n * LANES
                rows = pl.ds(at % rows_in + r, 8)
                out_ref[at // rows_in, 0, rows, lanes] = re
                out_ref[at // rows_in, 1, rows, lanes] = im
        return carry

    lax.fori_loop(0, LANES // 8, tile_out, 0)
    for d in range(strips):
        for c in range(2):
            out_ref[d, c, pl.ds(rows_in, HALO), :] = jnp.zeros((HALO, width), jnp.float32)
            if d > 0:
                out_ref[d, c, pl.ds(rows_in, 1), :] = out_ref[d - 1, c, pl.ds(rows_in - 1, 1), :]
            if d < strips - 1:
                out_ref[d, c, pl.ds(rows_in + 1, 1), :] = out_ref[d + 1, c, pl.ds(0, 1), :]


def finish_kernel(
    ang_ref, mean_ref, in_ref, src_ref, slow_ref, tw_ref, m_ref, *rest, member, batch_total
):
    if member:
        _, before_ref, out_ref, term_ref, zs, field = rest
    else:
        out_ref, term_ref, zs, field = rest
    factor, tall = zs.shape[0], zs.shape[1]
    rows_in, width = tall - HALO, in_ref.shape[3]
    block, full = term_ref.shape
    step = pl.program_id(0)

    @pl.when(step == 0)
    def _():
        for k in range(factor):
            at = k * LANES
            cols = pl.ds(at % width, LANES)
            x = jnp.concatenate(
                [in_ref[at // width, 0, :, cols], in_ref[at // width, 1, :, cols]], axis=1
            )
            high, low = split(x)
            zs[k] = dot(high, m_ref[0]) + (dot(low, m_ref[0]) + dot(high, m_ref[1]))

        def columns(rows):
            cells = []
            for k in range(factor):
                re, im = zs[k, rows, pl.ds(0, LANES)], zs[k, rows, pl.ds(LANES, LANES)]
                if k:
                    c, s = tw_ref[0, pl.ds(k, 1), :], tw_ref[1, pl.ds(k, 1), :]
                    re, im = re * c - im * s, im * c + re * s
                cells.append((re, im))
            return fft_list(cells, 1.0)

        def tile(t, carry):
            r = pl.multiple_of(t * 8, 8)
            for n, pair in enumerate(columns(pl.ds(r, 8))):
                for c in range(2):
                    field[c, pl.ds(8 + r, 8), pl.ds(n * LANES, LANES)] = pair[c]
            return carry

        lax.fori_loop(0, rows_in // 8, tile, 0)
        for n, pair in enumerate(columns(pl.ds(rows_in, 8))):
            for c in range(2):
                field[c, pl.ds(7, 1), pl.ds(n * LANES, LANES)] = pair[c][0:1]
                field[c, pl.ds(8 + rows_in, 1), pl.ds(n * LANES, LANES)] = pair[c][1:2]

    angular = ang_ref[member]
    ahead = 0.5 / (angular * mean_ref[0])
    column = lax.broadcasted_iota(jnp.int32, (block, full), 1)
    start = pl.multiple_of(step * block, 8)
    centre, laplace = [], []
    for c in range(2):
        cells = field[c, pl.ds(start, block + 16), :]
        mid = cells[8 : 8 + block]
        up = pltpu.roll(cells, 1, 0)[8 : 8 + block]
        down = pltpu.roll(cells, block + 15, 0)[8 : 8 + block]
        left = jnp.where(column == 0, 0.0, pltpu.roll(mid, 1, 1))
        right = jnp.where(column == full - 1, 0.0, pltpu.roll(mid, full - 1, 1))
        centre.append(mid)
        laplace.append(up + down + left + right - 4.0 * mid)
    slow = jnp.concatenate([slow_ref[p] for p in range(slow_ref.shape[0])], axis=1)
    gain = (ahead - 0.5 / (angular * slow)) * (depth_step / (grid_step * grid_step))
    new_re = centre[0] + gain * laplace[1]
    new_im = centre[1] - gain * laplace[0]
    out_ref[0, 0] = new_re
    out_ref[1, 0] = new_im
    term = (new_re * src_ref[0, 0] + new_im * src_ref[1, 0]) * (1.0 / math.sqrt(batch_total))
    term_ref[...] = term + before_ref[...] if member else term


def params():
    return pltpu.CompilerParams(vmem_limit_bytes=VMEM_BYTES)


def whole(array):
    zeros = (0,) * array.ndim
    return pl.BlockSpec(array.shape, lambda *_: zeros)


SMEM = pl.BlockSpec(memory_space=pltpu.SMEM)


def local(wavefield, source_field, slowness, freq_index):
    _, members, rows, full = wavefield.shape
    strips, groups = lax.axis_size("lat"), lax.axis_size("freq")
    width = full // strips
    factor = full // LANES
    part_width = full // groups
    count_x = rows * strips
    angular = 2.0 * math.pi * freq_step * freq_index.astype(jnp.float32)
    tw = twiddle(full)
    tw_row = jnp.asarray(tw)
    tw_x = jnp.asarray(np.ascontiguousarray(np.broadcast_to(tw[..., None], tw.shape + (LANES,))))
    right_fwd, right_inv = dft_tables(-1.0), dft_tables(1.0)
    m_fwd, m_inv = split_table(right_fwd), split_table(right_inv)
    m_both = jnp.concatenate(
        [split_table(np.ascontiguousarray(right_fwd.T)), split_table(np.ascontiguousarray(right_inv.T))]
    )
    strip = lax.all_gather(slowness, "freq", axis=0, tiled=False)

    block = 64

    def forward(member):
        return pl.pallas_call(
            functools.partial(forward_kernel, member=member),
            grid=(rows // block,),
            in_specs=[
                SMEM,
                pl.BlockSpec((2, 1, block, full), lambda i: (0, member, i, 0)),
                pl.BlockSpec((groups, block, part_width), lambda i: (0, i, 0)),
                whole(tw_row),
                whole(m_fwd),
            ],
            out_specs=pl.BlockSpec((strips, 2, block, width), lambda i: (0, 0, i, 0)),
            out_shape=jax.ShapeDtypeStruct((strips, 2, rows, width), jnp.float32),
            scratch_shapes=[pltpu.VMEM((factor, block, 2 * LANES), jnp.float32)],
            compiler_params=params(),
            cost_estimate=pl.CostEstimate(
                flops=4_000_000_000, bytes_accessed=40_000_000, transcendentals=0
            ),
            name="forward",
        )(angular, wavefield, strip, tw_row, m_fwd)

    def shift(member, mean_slow, spectra):
        return pl.pallas_call(
            functools.partial(shift_kernel, member=member),
            grid=(1,),
            in_specs=[SMEM, SMEM, whole(spectra), whole(tw_x), whole(m_both)],
            out_specs=pl.BlockSpec((strips, 2, rows + HALO, width), lambda i: (0, 0, 0, 0)),
            out_shape=jax.ShapeDtypeStruct((strips, 2, rows + HALO, width), jnp.float32),
            scratch_shapes=[pltpu.VMEM((factor, 2 * LANES, width), jnp.float32)],
            compiler_params=params(),
            cost_estimate=pl.CostEstimate(
                flops=10_000_000_000, bytes_accessed=100_000_000, transcendentals=0
            ),
            name="shift",
        )(angular, mean_slow, spectra, tw_x, m_both)

    final_block = 32

    def finish(member, mean_slow, lines, before):
        strip_block = pl.BlockSpec((groups, final_block, part_width), lambda i: (0, i, 0))
        term_block = pl.BlockSpec((final_block, full), lambda i: (i, 0))
        field_block = pl.BlockSpec((2, 1, final_block, full), lambda i: (0, member, i, 0))
        specs = [SMEM, SMEM, whole(lines), field_block, strip_block, whole(tw_row), whole(m_inv)]
        arrays = [angular, mean_slow, lines, source_field, strip, tw_row, m_inv]
        aliases = {}
        if member:
            aliases = {len(arrays): 0}
            specs += [pl.BlockSpec(memory_space=pl.ANY), term_block]
            arrays += list(before)
        return pl.pallas_call(
            functools.partial(
                finish_kernel, member=member, batch_total=members * groups
            ),
            grid=(rows // final_block,),
            in_specs=specs,
            out_specs=[field_block, term_block],
            out_shape=[
                jax.ShapeDtypeStruct((2, members, rows, full), jnp.float32),
                jax.ShapeDtypeStruct((rows, full), jnp.float32),
            ],
            scratch_shapes=[
                pltpu.VMEM((factor, rows + HALO, 2 * LANES), jnp.float32),
                pltpu.VMEM((2, rows + 16, full), jnp.float32),
            ],
            input_output_aliases=aliases,
            compiler_params=params(),
            cost_estimate=pl.CostEstimate(
                flops=8_000_000_000, bytes_accessed=80_000_000, transcendentals=0
            ),
            name="finish",
        )(*arrays)

    def exchange(cells):
        return lax.all_to_all(cells, "lat", split_axis=0, concat_axis=0, tiled=True)

    spectra = [forward(m) for m in range(members)]
    later, spectra[-1] = lax.optimization_barrier((slowness, spectra[-1]))
    total = lax.psum(jnp.sum(later), ("lat", "freq"))
    mean_slow = (total / (count_x * full)).reshape(1)
    lines = [exchange(s) for s in spectra]
    shifted = [exchange(shift(m, mean_slow, lines[m])) for m in range(members)]
    state = None
    for m in range(members):
        state = finish(m, mean_slow, shifted[m], state)
    field, terms = state
    image = lax.psum_scatter(terms, "freq", scatter_dimension=1, tiled=True)
    return (field, image)


def solution(mesh):
    return jax.shard_map(
        local,
        mesh=mesh,
        in_specs=(
            P(None, "freq", "lat", None),
            P(None, "freq", "lat", None),
            P("lat", "freq"),
            P("freq"),
        ),
        out_specs=(P(None, "freq", "lat", None), P("lat", "freq")),
        check_vma=False,
    )
```

time: 933 us -> 561 us (0.60)
  matrix products: 241 us -> 0 us
  local copies, waits for them, and re-layouts: 156 us -> 9.17 us
  blocking collectives: 17 us -> 113 us
  other arithmetic: 95.3 us -> 1.39 us
  Pallas kernels: 0 us -> 87.7 us
  waiting for transfers between devices: 388 us -> 316 us
    dot_general x32 -> x0, matrix products: 241 us -> none  [the longest x8 62.6 us: table_product(): jnp.einsum(form, cos_t, real, precision=highest)]
    all_to_all x2 -> x4, waiting for transfers between devices: 349 us -> 241 us  [exchange(): return lax.all_to_all(cells, 'lat', split_axis=0, concat_axis=0, tiled=True)]
    psum x1, blocking collectives: 17 us -> 113 us  [local(): total = lax.psum(jnp.sum(later), ('lat', 'freq'))]
    pallas_call x0 -> x6, Pallas kernels: none -> 87.7 us  [the longest x2 42.3 us: shift(): pl.pallas_call(functools.partial(shift_kernel, member=member), grid=(1,),...]
    sub x5 -> x0, other arithmetic: 59.1 us -> none  [the longest x1 21.9 us: local(): laplace = beside_all - 4.0 * stacked]
    slice x10 -> x0, local copies, waits for them, and re-layouts: 51 us -> none  [the longest x3 14.9 us: spectral_step(): spec_real, spec_imag = transform_axis(columns[0], columns[1], -1.0, True)]
    another operation x2 -> x0, local copies, waits for them, and re-layouts: 33.2 us -> none  [the longest x1 16.7 us: spectral_step(): jnp.stack([back_real, back_imag])]
    unnamed x41 -> x26, local copies, waits for them, and re-layouts: 36.1 us -> 9.17 us
  transfers between devices with their start and end apart: 6 -> 6, of which waited for: 4 -> 5; matrix products, arithmetic and copies ran while one was open for 7% -> 0% of each run, Pallas kernels for 0% -> 12%
where the time goes in v1:
time: 561 us; the launch traced here: 560 us
  waiting for transfers between devices  316 us (56%)
  blocking collectives  113 us (20%)
  Pallas kernels  87.7 us (16%)
  starting transfers between devices  18.6 us (3%)
  between operations  14.8 us (3%)
  local copies, waits for them, and re-layouts  9.17 us (2%)
    all_to_all x4, waiting for transfers between devices, exchange(): return lax.all_to_all(cells, 'lat', split_axis=0, concat_axis=0, tiled=True)  241 us
    psum x1, blocking collectives, local(): total = lax.psum(jnp.sum(later), ('lat', 'freq'))  113 us
    pallas_call x2, Pallas kernels, shift(): pl.pallas_call(functools.partial(shift_kernel, member=member), grid=(1,),...  42.3 us
    all_gather x1, waiting for transfers between devices, local(): strip = lax.all_gather(slowness, 'freq', axis=0, tiled=False)  39.3 us
    reduce_scatter x1, waiting for transfers between devices, local(): image = lax.psum_scatter(terms, 'freq', scatter_dimension=1, tiled=True)  35.2 us
    pallas_call x2, Pallas kernels, finish(): pl.pallas_call(functools.partial(finish_kernel, member=member, batch_tota...  26.3 us
    pallas_call x2, Pallas kernels, forward(): pl.pallas_call(functools.partial(forward_kernel, member=member), grid=(ro...  19 us
    all_to_all x4, starting transfers between devices, exchange(): return lax.all_to_all(cells, 'lat', split_axis=0, concat_axis=0, tiled=True)  18.5 us
  transfers between devices with their start and end apart: 6, of which 5 were waited for; matrix products, arithmetic and copies ran while one was open for 0% of the time, Pallas kernels for 12%

profile of v1, /device:TPU:0, one launch (start us, length us, event | category | flops | bytes accessed | tf_op | source)
XLA Modules:
  0.0 560.3 jit_solution(6914551944475265144)
XLA Ops:
  8.6 39.3 %all-gather.3.cloned.1.call-done = f32[1024,512]{1,0:T(8,128)} async-done(((f32[256,512]{1,0:T(8,128)}), f32[1024,512]{1,0:T(8,128)}) %all-gather.3.cloned.1.call-update) | async-done | bytes 2097168 | tf_op jit(solution)/shard_map/all_gather | solution.py:308
  47.9 1.6 copy-done
  49.5 0.9 copy-done.3
  50.4 0.7 copy-done.5
  51.1 9.5 %forward.3 = f32[8,2,256,256]{3,2,1,0:T(8,128)} custom-call(f32[2]{0:T(128)S(1)} %convert_multiply_fusion.ang_ref, f32[2,2,256,2048]{3,2,1,0:T(8,128)} %wave_ref.3, f32[4,256,512]{2,1,0:T(8,128)S(1)} %bitcast.2, f32[2,16,128]{2,1,0:T(8,128)S(1)} %copy-done.5, bf16[2,256,256]{2,1,0:T(8,128)(2,1)S(1)} %copy-done.3), custom_call_target="tpu_custom_call" | custom-call | flops 4000000000 | bytes 40000000 | tf_op jit(solution)/shard_map/forward/pallas_call | solution.py:313
  60.6 4.7 all-to-all-start.2
  65.4 9.5 %forward.2 = f32[8,2,256,256]{3,2,1,0:T(8,128)} custom-call(f32[2]{0:T(128)S(1)} %convert_multiply_fusion.ang_ref, f32[2,2,256,2048]{3,2,1,0:T(8,128)} %wave_ref.3, f32[4,256,512]{2,1,0:T(8,128)S(1)} %bitcast.3, f32[2,16,128]{2,1,0:T(8,128)S(1)} %copy-done.6, bf16[2,256,256]{2,1,0:T(8,128)(2,1)S(1)} %copy-done.4), custom_call_target="tpu_custom_call" | custom-call | flops 4000000000 | bytes 40000000 | tf_op jit(solution)/shard_map/forward/pallas_call | solution.py:313
  75.0 84.5 %all-to-all-done.2.in_ref = f32[8,2,256,256]{3,2,1,0:T(8,128)} async-done(((f32[8,2,256,256]{3,2,1,0:T(8,128)}), f32[8,2,256,256]{3,2,1,0:T(8,128)}, u32[]{:S(2)}, u32[]{:S(2)}) %all-to-all-start.2) | async-done | bytes 4194336 | tf_op jit(solution)/shard_map/all_to_all | solution.py:385
  159.5 4.6 all-to-all-start
  164.1 0.7 reduce_sum.9
  164.8 112.5 %psum.7 = f32[]{:T(128)} all-reduce(f32[]{:T(128)} %reduce_sum.9), channel_id=1, replica_groups=mesh['lat'=8,'freq'=4] {'lat','freq'}, use_global_device_ids=true, to_apply=%region_1.0 | all-reduce | flops 1 | bytes 8 | tf_op jit(solution)/shard_map/psum | solution.py:389
  278.0 1.6 copy-done.7
  279.6 21.2 %shift.3 = f32[8,2,264,256]{3,2,1,0:T(8,128)} custom-call(f32[2]{0:T(128)S(1)} %convert_multiply_fusion.ang_ref, f32[1]{0:T(128)} %bitcast.1.mean_ref, f32[8,2,256,256]{3,2,1,0:T(8,128)} %all-to-all-done.2.in_ref, f32[2,16,128,128]{3,2,1,0:T(8,128)S(1)} %copy-done.7, bf16[4,256,256]{2,1,0:T(8,128)(2,1)S(1)} %copy-done.9), custom_call_target="tpu_custom_call" | custom-call | flops 10000000000 | bytes 100000000 | tf_op jit(solution)/shard_map/shift/pallas_call | solution.py:334
  300.8 4.6 all-to-all-start.3
  305.4 1.6 copy-done.8
  307.0 21.1 %shift.2 = f32[8,2,264,256]{3,2,1,0:T(8,128)} custom-call(f32[2]{0:T(128)S(1)} %convert_multiply_fusion.ang_ref, f32[1]{0:T(128)} %bitcast.1.mean_ref, f32[8,2,256,256]{3,2,1,0:T(8,128)} %all-to-all-done.in_ref, f32[2,16,128,128]{3,2,1,0:T(8,128)S(1)} %copy-done.8, bf16[4,256,256]{2,1,0:T(8,128)(2,1)S(1)} %copy-done.9), custom_call_target="tpu_custom_call" | custom-call | flops 10000000000 | bytes 100000000 | tf_op jit(solution)/shard_map/shift/pallas_call | solution.py:334
  328.1 74.1 %all-to-all-done.3.in_ref = f32[8,2,264,256]{3,2,1,0:T(8,128)} async-done(((f32[8,2,264,256]{3,2,1,0:T(8,128)}), f32[8,2,264,256]{3,2,1,0:T(8,128)}, u32[]{:S(2)}, u32[]{:S(2)}) %all-to-all-start.3) | async-done | bytes 4325408 | tf_op jit(solution)/shard_map/all_to_all | solution.py:385
  402.2 4.6 all-to-all-start.1
  406.9 13.0 %finish.2 = (f32[2,2,256,2048]{3,2,1,0:T(8,128)}, f32[256,2048]{1,0:T(8,128)S(1)}) custom-call(f32[2]{0:T(128)S(1)} %convert_multiply_fusion.ang_ref, f32[1]{0:T(128)} %bitcast.1.mean_ref, f32[8,2,264,256]{3,2,1,0:T(8,128)} %all-to-all-done.3.in_ref, f32[2,2,256,2048]{3,2,1,0:T(8,128)} %src_ref.3, f32[4,256,512]{2,1,0:T(8,128)S(1)} %bitcast.4, ...), custom_call_target="tpu_custom_call" | custom-call | flops 8000000000 | bytes 80000000 | tf_op jit(solution)/shard_map/finish/pallas_call | solution.py:361
  419.8 1.4 copy-done.11
  421.2 82.4 %all-to-all-done.1.in_ref = f32[8,2,264,256]{3,2,1,0:T(8,128)} async-done(((f32[8,2,264,256]{3,2,1,0:T(8,128)}), f32[8,2,264,256]{3,2,1,0:T(8,128)}, u32[]{:S(2)}, u32[]{:S(2)}) %all-to-all-start.1) | async-done | bytes 4325408 | tf_op jit(solution)/shard_map/all_to_all | solution.py:385
  503.6 13.4 %finish.3 = (f32[2,2,256,2048]{3,2,1,0:T(8,128)}, f32[256,2048]{1,0:T(8,128)S(1)}) custom-call(f32[2]{0:T(128)S(1)} %convert_multiply_fusion.ang_ref, f32[1]{0:T(128)} %bitcast.1.mean_ref, f32[8,2,264,256]{3,2,1,0:T(8,128)} %all-to-all-done.1.in_ref, f32[2,2,256,2048]{3,2,1,0:T(8,128)} %src_ref.3, ...), custom_call_target="tpu_custom_call", output_to_operand_aliasing={{0}: (7, {})} | custom-call | flops 8000000000 | bytes 80000000 | tf_op jit(solution)/shard_map/finish/pallas_call | solution.py:361
  517.0 1.3 copy-done.2
  518.3 35.2 %reduce-scatter.2.cloned.1.call-done = f32[256,512]{1,0:T(8,128)} async-done(((f32[256,2048]{1,0:T(8,128)}), f32[256,512]{1,0:T(8,128)}) %reduce-scatter.2.cloned.1.call-update) | async-done | bytes 524304 | tf_op jit(solution)/shard_map/reduce_scatter | solution.py:397
  (25 shorter events, 1.5 us)
Async XLA Ops:
  7.2 40.7 %all-gather.3.cloned.1.call-start = ((), (), s32[]{:S(2)}) async-start(), calls=%async_computation.6 | async-start | bytes 2621440 | tf_op jit(solution)/shard_map/all_gather | solution.py:308
  47.9 1.6 copy-start
  49.5 0.9 copy-start.3
  50.4 0.7 copy-start.5
  60.6 4.8 copy-start.1
  60.6 4.8 copy-start.4
  60.6 4.8 copy-start.6
  60.6 98.9 %all-to-all-start.2 = ((f32[8,2,256,256]{3,2,1,0:T(8,128)}), f32[8,2,256,256]{3,2,1,0:T(8,128)}, u32[]{:S(2)}, u32[]{:S(2)}) async-start(f32[8,2,256,256]{3,2,1,0:T(8,128)} %forward.3), calls=%async_computation.2 | async-start | bytes 8388608 | tf_op jit(solution)/shard_map/all_to_all | solution.py:385
  74.9 89.1 %copy-start.12 = (f32[256,512]{1,0:T(8,128)S(1)}, f32[256,512]{1,0:T(8,128)}, u32[]{:S(2)}) copy-start(f32[256,512]{1,0:T(8,128)} %param.16) | copy-start | bytes 1572868
  74.9 203.0 %copy-start.9 = (bf16[4,256,256]{2,1,0:T(8,128)(2,1)S(1)}, bf16[4,256,256]{2,1,0:T(8,128)(2,1)}, u32[]{:S(2)}) copy-start(bf16[4,256,256]{2,1,0:T(8,128)(2,1)} %constant.35.m_ref) | copy-start | bytes 1572868
  159.5 141.3 %all-to-all-start = ((f32[8,2,256,256]{3,2,1,0:T(8,128)}), f32[8,2,256,256]{3,2,1,0:T(8,128)}, u32[]{:S(2)}, u32[]{:S(2)}) async-start(f32[8,2,256,256]{3,2,1,0:T(8,128)} %forward.2), calls=%async_computation | async-start | bytes 8388608 | tf_op jit(solution)/shard_map/all_to_all | solution.py:385
  278.0 1.6 copy-start.7
  300.8 101.4 %all-to-all-start.3 = ((f32[8,2,264,256]{3,2,1,0:T(8,128)}), f32[8,2,264,256]{3,2,1,0:T(8,128)}, u32[]{:S(2)}, u32[]{:S(2)}) async-start(f32[8,2,264,256]{3,2,1,0:T(8,128)} %shift.3), calls=%async_computation.3 | async-start | bytes 8650752 | tf_op jit(solution)/shard_map/all_to_all | solution.py:385
  305.4 1.6 copy-start.8
  328.1 78.7 %copy-start.10 = (bf16[2,256,256]{2,1,0:T(8,128)(2,1)S(1)}, bf16[2,256,256]{2,1,0:T(8,128)(2,1)}, u32[]{:S(2)}) copy-start(bf16[2,256,256]{2,1,0:T(8,128)(2,1)} %constant.36.m_ref) | copy-start | bytes 786436
  402.2 101.4 %all-to-all-start.1 = ((f32[8,2,264,256]{3,2,1,0:T(8,128)}), f32[8,2,264,256]{3,2,1,0:T(8,128)}, u32[]{:S(2)}, u32[]{:S(2)}) async-start(f32[8,2,264,256]{3,2,1,0:T(8,128)} %shift.2), calls=%async_computation.1 | async-start | bytes 8650752 | tf_op jit(solution)/shard_map/all_to_all | solution.py:385
  406.8 146.7 %reduce-scatter.2.cloned.1.call-start = ((), (), s32[]{:S(2)}) async-start(), calls=%async_computation.5 | async-start | bytes 2621440 | tf_op jit(solution)/shard_map/reduce_scatter | solution.py:397
  419.8 1.4 copy-start.11
  517.0 1.3 copy-start.2
Sparse Core Ops, SparseCore 0:
  9.8 38.0 all-gather.2
  518.5 34.9 reduce-scatter.1

commit v2 on v1

--- a/solution.py
+++ b/solution.py
@@ -151,7 +151,7 @@
 
     lax.fori_loop(0, LANES // 8, tile_in, 0)
 
-    flat = angular_mean = ang_ref[member] * mean_ref[0]
+    angular_mean = ang_ref[member] * mean_ref[0]
     flat = angular_mean * depth_step
     place = base + lax.broadcasted_iota(jnp.int32, (LANES, width), 1)
     index_y = place // LANES + factor * (place % LANES)
@@ -216,7 +216,8 @@
         out_ref, term_ref, zs, field = rest
     factor, tall = zs.shape[0], zs.shape[1]
     rows_in, width = tall - HALO, in_ref.shape[3]
-    block, full = term_ref.shape
+    block, part_width = term_ref.shape[1:]
+    full = field.shape[2]
     step = pl.program_id(0)
 
     @pl.when(step == 0)
@@ -274,7 +275,9 @@
     out_ref[0, 0] = new_re
     out_ref[1, 0] = new_im
     term = (new_re * src_ref[0, 0] + new_im * src_ref[1, 0]) * (1.0 / math.sqrt(batch_total))
-    term_ref[...] = term + before_ref[...] if member else term
+    for p in range(slow_ref.shape[0]):
+        part = term[:, p * part_width : (p + 1) * part_width]
+        term_ref[p] = part + before_ref[p] if member else part
 
 
 def params():
@@ -305,7 +308,11 @@
     m_both = jnp.concatenate(
         [split_table(np.ascontiguousarray(right_fwd.T)), split_table(np.ascontiguousarray(right_inv.T))]
     )
-    strip = lax.all_gather(slowness, "freq", axis=0, tiled=False)
+    total = lax.psum(jnp.sum(slowness), ("lat", "freq"))
+    copies = jnp.broadcast_to(slowness, (groups,) + slowness.shape)
+    strip = lax.all_to_all(copies, "freq", split_axis=0, concat_axis=0, tiled=True)
+    strip, total = lax.optimization_barrier((strip, total))
+    mean_slow = (total / (count_x * full)).reshape(1)
 
     block = 64
 
@@ -349,14 +356,13 @@
 
     def finish(member, mean_slow, lines, before):
         strip_block = pl.BlockSpec((groups, final_block, part_width), lambda i: (0, i, 0))
-        term_block = pl.BlockSpec((final_block, full), lambda i: (i, 0))
         field_block = pl.BlockSpec((2, 1, final_block, full), lambda i: (0, member, i, 0))
         specs = [SMEM, SMEM, whole(lines), field_block, strip_block, whole(tw_row), whole(m_inv)]
         arrays = [angular, mean_slow, lines, source_field, strip, tw_row, m_inv]
         aliases = {}
         if member:
             aliases = {len(arrays): 0}
-            specs += [pl.BlockSpec(memory_space=pl.ANY), term_block]
+            specs += [pl.BlockSpec(memory_space=pl.ANY), strip_block]
             arrays += list(before)
         return pl.pallas_call(
             functools.partial(
@@ -364,10 +370,10 @@
             ),
             grid=(rows // final_block,),
             in_specs=specs,
-            out_specs=[field_block, term_block],
+            out_specs=[field_block, strip_block],
             out_shape=[
                 jax.ShapeDtypeStruct((2, members, rows, full), jnp.float32),
-                jax.ShapeDtypeStruct((rows, full), jnp.float32),
+                jax.ShapeDtypeStruct((groups, rows, part_width), jnp.float32),
             ],
             scratch_shapes=[
                 pltpu.VMEM((factor, rows + HALO, 2 * LANES), jnp.float32),
@@ -385,16 +391,15 @@
         return lax.all_to_all(cells, "lat", split_axis=0, concat_axis=0, tiled=True)
 
     spectra = [forward(m) for m in range(members)]
-    later, spectra[-1] = lax.optimization_barrier((slowness, spectra[-1]))
-    total = lax.psum(jnp.sum(later), ("lat", "freq"))
-    mean_slow = (total / (count_x * full)).reshape(1)
     lines = [exchange(s) for s in spectra]
     shifted = [exchange(shift(m, mean_slow, lines[m])) for m in range(members)]
     state = None
     for m in range(members):
         state = finish(m, mean_slow, shifted[m], state)
     field, terms = state
-    image = lax.psum_scatter(terms, "freq", scatter_dimension=1, tiled=True)
+    image = jnp.sum(
+        lax.all_to_all(terms, "freq", split_axis=0, concat_axis=0, tiled=True), axis=0
+    )
     return (field, image)
 
 

time: 561 us -> 522 us (0.930)
  blocking collectives: 113 us -> 87.4 us
  between operations: 14.8 us -> 1.4 us
    all_to_all x4, waiting for transfers between devices: 241 us -> 312 us  [exchange(): return lax.all_to_all(cells, 'lat', split_axis=0, concat_axis=0, tiled=True)]
    psum x1, blocking collectives: 113 us -> 58.6 us  [local(): total = lax.psum(jnp.sum(slowness), ('lat', 'freq'))]
    all_gather x1 -> x0, waiting for transfers between devices: 39.3 us -> none  [local(): strip = lax.all_gather(slowness, 'freq', axis=0, tiled=False)]
    reduce_scatter x1 -> x0, waiting for transfers between devices: 35.2 us -> none  [local(): image = lax.psum_scatter(terms, 'freq', scatter_dimension=1, tiled=True)]
    all_to_all x0 -> x1, blocking collectives: none -> 28.7 us  [local(): lax.all_to_all(terms, 'freq', split_axis=0, concat_axis=0, tiled=True)]
  transfers between devices with their start and end apart: 6 -> 5, of which waited for: 5 -> 4; matrix products, arithmetic and copies ran while one was open for 0% -> 0% of each run, Pallas kernels for 12% -> 12%
where the time goes in v2:
time: 522 us; the launch traced here: 521 us
  waiting for transfers between devices  312 us (60%)
  Pallas kernels  87.8 us (17%)
  blocking collectives  87.4 us (17%)
  starting transfers between devices  23.5 us (5%)
  local copies, waits for them, and re-layouts  7.29 us (1%)
    all_to_all x4, waiting for transfers between devices, exchange(): return lax.all_to_all(cells, 'lat', split_axis=0, concat_axis=0, tiled=True)  312 us
    psum x1, blocking collectives, local(): total = lax.psum(jnp.sum(slowness), ('lat', 'freq'))  58.6 us
    pallas_call x2, Pallas kernels, shift(): pl.pallas_call(functools.partial(shift_kernel, member=member), grid=(1,),...  42.3 us
    all_to_all x1, blocking collectives, local(): lax.all_to_all(terms, 'freq', split_axis=0, concat_axis=0, tiled=True)  28.7 us
    pallas_call x2, Pallas kernels, finish(): pl.pallas_call(functools.partial(finish_kernel, member=member, batch_tota...  26.4 us
    pallas_call x2, Pallas kernels, forward(): pl.pallas_call(functools.partial(forward_kernel, member=member), grid=(ro...  19 us
    all_to_all x4, starting transfers between devices, exchange(): return lax.all_to_all(cells, 'lat', split_axis=0, concat_axis=0, tiled=True)  18.3 us
  transfers between devices with their start and end apart: 5, of which 4 were waited for; matrix products, arithmetic and copies ran while one was open for 0% of the time, Pallas kernels for 12%

profile of v2, /device:TPU:0, one launch (start us, length us, event | category | flops | bytes accessed | tf_op | source)
XLA Modules:
  0.0 520.6 jit_solution(6989774604019153264)
XLA Ops:
  0.6 0.0 copy-start.1
  0.7 2.7 broadcast_in_dim.3
  3.4 5.2 all-to-all-start
  8.5 0.7 reduce_sum.18
  9.3 58.6 %psum.7 = f32[]{:T(128)} all-reduce(f32[]{:T(128)} %reduce_sum.18), channel_id=1, replica_groups=mesh['lat'=8,'freq'=4] {'lat','freq'}, use_global_device_ids=true, to_apply=%region_1.0 | all-reduce | flops 1 | bytes 8 | tf_op jit(solution)/shard_map/psum | solution.py:311
  68.0 9.5 %forward.3 = f32[8,2,256,256]{3,2,1,0:T(8,128)} custom-call(f32[2]{0:T(128)S(1)} %convert_multiply_fusion.ang_ref, f32[2,2,256,2048]{3,2,1,0:T(8,128)} %wave_ref.3, f32[4,256,512]{2,1,0:T(8,128)S(1)} %all-to-all-done.slow_ref, f32[2,16,128]{2,1,0:T(8,128)S(1)} %copy-done.1, bf16[2,256,256]{2,1,0:T(8,128)(2,1)S(1)} %copy-done), custom_call_target="tpu_custom_call" | custom-call | flops 4000000000 | bytes 40000000 | tf_op jit(solution)/shard_map/forward/pallas_call | solution.py:320
  77.4 4.6 all-to-all-start.3
  82.0 9.5 %forward.2 = f32[8,2,256,256]{3,2,1,0:T(8,128)} custom-call(f32[2]{0:T(128)S(1)} %convert_multiply_fusion.ang_ref, f32[2,2,256,2048]{3,2,1,0:T(8,128)} %wave_ref.3, f32[4,256,512]{2,1,0:T(8,128)S(1)} %all-to-all-done.slow_ref, f32[2,16,128]{2,1,0:T(8,128)S(1)} %copy-done.1, bf16[2,256,256]{2,1,0:T(8,128)(2,1)S(1)} %copy-done), custom_call_target="tpu_custom_call" | custom-call | flops 4000000000 | bytes 40000000 | tf_op jit(solution)/shard_map/forward/pallas_call | solution.py:320
  91.5 84.5 %all-to-all-done.3.in_ref = f32[8,2,256,256]{3,2,1,0:T(8,128)} async-done(((f32[8,2,256,256]{3,2,1,0:T(8,128)}), f32[8,2,256,256]{3,2,1,0:T(8,128)}, u32[]{:S(2)}, u32[]{:S(2)}) %all-to-all-start.3) | async-done | bytes 4194336 | tf_op jit(solution)/shard_map/all_to_all | solution.py:391
  176.0 4.6 all-to-all-start.1
  181.2 1.6 copy-done.2
  182.8 21.2 %shift.3 = f32[8,2,264,256]{3,2,1,0:T(8,128)} custom-call(f32[2]{0:T(128)S(1)} %convert_multiply_fusion.ang_ref, f32[1]{0:T(128)} %bitcast.mean_ref, f32[8,2,256,256]{3,2,1,0:T(8,128)} %all-to-all-done.3.in_ref, f32[2,16,128,128]{3,2,1,0:T(8,128)S(1)} %copy-done.2, bf16[4,256,256]{2,1,0:T(8,128)(2,1)S(1)} %copy-done.4), custom_call_target="tpu_custom_call" | custom-call | flops 10000000000 | bytes 100000000 | tf_op jit(solution)/shard_map/shift/pallas_call | solution.py:341
  204.0 70.6 %all-to-all-done.1.in_ref = f32[8,2,256,256]{3,2,1,0:T(8,128)} async-done(((f32[8,2,256,256]{3,2,1,0:T(8,128)}), f32[8,2,256,256]{3,2,1,0:T(8,128)}, u32[]{:S(2)}, u32[]{:S(2)}) %all-to-all-start.1) | async-done | bytes 4194336 | tf_op jit(solution)/shard_map/all_to_all | solution.py:391
  274.6 4.6 all-to-all-start.4
  279.2 1.6 copy-done.3
  280.8 21.1 %shift.2 = f32[8,2,264,256]{3,2,1,0:T(8,128)} custom-call(f32[2]{0:T(128)S(1)} %convert_multiply_fusion.ang_ref, f32[1]{0:T(128)} %bitcast.mean_ref, f32[8,2,256,256]{3,2,1,0:T(8,128)} %all-to-all-done.1.in_ref, f32[2,16,128,128]{3,2,1,0:T(8,128)S(1)} %copy-done.3, bf16[4,256,256]{2,1,0:T(8,128)(2,1)S(1)} %copy-done.4), custom_call_target="tpu_custom_call" | custom-call | flops 10000000000 | bytes 100000000 | tf_op jit(solution)/shard_map/shift/pallas_call | solution.py:341
  302.0 74.1 %all-to-all-done.4.in_ref = f32[8,2,264,256]{3,2,1,0:T(8,128)} async-done(((f32[8,2,264,256]{3,2,1,0:T(8,128)}), f32[8,2,264,256]{3,2,1,0:T(8,128)}, u32[]{:S(2)}, u32[]{:S(2)}) %all-to-all-start.4) | async-done | bytes 4325408 | tf_op jit(solution)/shard_map/all_to_all | solution.py:391
  376.1 4.6 all-to-all-start.2
  380.6 13.0 %finish.2 = (f32[2,2,256,2048]{3,2,1,0:T(8,128)}, f32[4,256,512]{2,1,0:T(8,128)S(1)}) custom-call(f32[2]{0:T(128)S(1)} %convert_multiply_fusion.ang_ref, f32[1]{0:T(128)} %bitcast.mean_ref, f32[8,2,264,256]{3,2,1,0:T(8,128)} %all-to-all-done.4.in_ref, f32[2,2,256,2048]{3,2,1,0:T(8,128)} %src_ref.3, f32[4,256,512]{2,1,0:T(8,128)S(1)} %all-to-all-done.slow_ref, ...), custom_call_target="tpu_custom_call" | custom-call | flops 8000000000 | bytes 80000000 | tf_op jit(solution)/shard_map/finish/pallas_call | solution.py:367
  393.7 1.4 copy-done.6
  395.0 82.4 %all-to-all-done.2.in_ref = f32[8,2,264,256]{3,2,1,0:T(8,128)} async-done(((f32[8,2,264,256]{3,2,1,0:T(8,128)}), f32[8,2,264,256]{3,2,1,0:T(8,128)}, u32[]{:S(2)}, u32[]{:S(2)}) %all-to-all-start.2) | async-done | bytes 4325408 | tf_op jit(solution)/shard_map/all_to_all | solution.py:391
  477.4 13.4 %finish.3 = (f32[2,2,256,2048]{3,2,1,0:T(8,128)}, f32[4,256,512]{2,1,0:T(8,128)S(1)}) custom-call(f32[2]{0:T(128)S(1)} %convert_multiply_fusion.ang_ref, f32[1]{0:T(128)} %bitcast.mean_ref, f32[8,2,264,256]{3,2,1,0:T(8,128)} %all-to-all-done.2.in_ref, f32[2,2,256,2048]{3,2,1,0:T(8,128)} %src_ref.3, ...), custom_call_target="tpu_custom_call", output_to_operand_aliasing={{0}: (7, {})} | custom-call | flops 8000000000 | bytes 80000000 | tf_op jit(solution)/shard_map/finish/pallas_call | solution.py:367
  490.8 28.7 %all_to_all.30 = f32[4,256,512]{2,1,0:T(8,128)S(1)} all-to-all(f32[4,256,512]{2,1,0:T(8,128)S(1)} %get-tuple-element.13), channel_id=1, replica_groups=mesh['lat'=8,'freq'=4] {'freq'}, dimensions={0} | all-to-all | bytes 4194304 | tf_op jit(solution)/shard_map/all_to_all | solution.py:401
  519.6 1.0 reduce_sum.19
  (16 shorter events, 0.0 us)
Async XLA Ops:
  0.6 67.3 %copy-start.1 = (f32[2,16,128]{2,1,0:T(8,128)S(1)}, f32[2,16,128]{2,1,0:T(8,128)}, u32[]{:S(2)}) copy-start(f32[2,16,128]{2,1,0:T(8,128)} %constant.19.clone.tw_ref) | copy-start | bytes 49156
  0.6 67.3 %copy-start = (bf16[2,256,256]{2,1,0:T(8,128)(2,1)S(1)}, bf16[2,256,256]{2,1,0:T(8,128)(2,1)}, u32[]{:S(2)}) copy-start(bf16[2,256,256]{2,1,0:T(8,128)(2,1)} %constant.31.m_ref) | copy-start | bytes 786436
  0.7 7.9 %copy-start.7 = (f32[256,512]{1,0:T(8,128)S(1)}, f32[256,512]{1,0:T(8,128)}, u32[]{:S(2)}) copy-start(f32[256,512]{1,0:T(8,128)} %param.16) | copy-start | bytes 1572868
  0.7 67.3 %copy-start.8 = (s32[2]{0:T(128)S(1)}, s32[2]{0:T(128)}, u32[]{:S(2)}) copy-start(s32[2]{0:T(128)} %param.17) | copy-start | bytes 28
  3.4 64.6 %all-to-all-start = ((f32[4,256,512]{2,1,0:T(8,128)}), f32[4,256,512]{2,1,0:T(8,128)S(1)}, u32[]{:S(2)}, u32[]{:S(2)}) async-start(f32[4,256,512]{2,1,0:T(8,128)} %broadcast_in_dim.3), calls=%async_computation | async-start | bytes 4194304 | tf_op jit(solution)/shard_map/all_to_all | solution.py:313
  77.4 98.6 %all-to-all-start.3 = ((f32[8,2,256,256]{3,2,1,0:T(8,128)}), f32[8,2,256,256]{3,2,1,0:T(8,128)}, u32[]{:S(2)}, u32[]{:S(2)}) async-start(f32[8,2,256,256]{3,2,1,0:T(8,128)} %forward.3), calls=%async_computation.3 | async-start | bytes 8388608 | tf_op jit(solution)/shard_map/all_to_all | solution.py:391
  91.5 89.7 %copy-start.4 = (bf16[4,256,256]{2,1,0:T(8,128)(2,1)S(1)}, bf16[4,256,256]{2,1,0:T(8,128)(2,1)}, u32[]{:S(2)}) copy-start(bf16[4,256,256]{2,1,0:T(8,128)(2,1)} %constant.35.m_ref) | copy-start | bytes 1572868
  176.0 98.6 %all-to-all-start.1 = ((f32[8,2,256,256]{3,2,1,0:T(8,128)}), f32[8,2,256,256]{3,2,1,0:T(8,128)}, u32[]{:S(2)}, u32[]{:S(2)}) async-start(f32[8,2,256,256]{3,2,1,0:T(8,128)} %forward.2), calls=%async_computation.1 | async-start | bytes 8388608 | tf_op jit(solution)/shard_map/all_to_all | solution.py:391
  181.2 1.6 copy-start.2
  274.6 101.5 %all-to-all-start.4 = ((f32[8,2,264,256]{3,2,1,0:T(8,128)}), f32[8,2,264,256]{3,2,1,0:T(8,128)}, u32[]{:S(2)}, u32[]{:S(2)}) async-start(f32[8,2,264,256]{3,2,1,0:T(8,128)} %shift.3), calls=%async_computation.4 | async-start | bytes 8650752 | tf_op jit(solution)/shard_map/all_to_all | solution.py:391
  279.2 1.6 copy-start.3
  302.0 78.7 %copy-start.5 = (bf16[2,256,256]{2,1,0:T(8,128)(2,1)S(1)}, bf16[2,256,256]{2,1,0:T(8,128)(2,1)}, u32[]{:S(2)}) copy-start(bf16[2,256,256]{2,1,0:T(8,128)(2,1)} %constant.36.m_ref) | copy-start | bytes 786436
  376.1 101.4 %all-to-all-start.2 = ((f32[8,2,264,256]{3,2,1,0:T(8,128)}), f32[8,2,264,256]{3,2,1,0:T(8,128)}, u32[]{:S(2)}, u32[]{:S(2)}) async-start(f32[8,2,264,256]{3,2,1,0:T(8,128)} %shift.2), calls=%async_computation.2 | async-start | bytes 8650752 | tf_op jit(solution)/shard_map/all_to_all | solution.py:391
  393.7 1.4 copy-start.6

commit v3 on v2

--- a/solution.py
+++ b/solution.py
@@ -89,17 +89,25 @@
     return jnp.dot(a, b, preferred_element_type=jnp.float32)
 
 
-def forward_kernel(ang_ref, wave_ref, slow_ref, tw_ref, m_ref, out_ref, zs, *, member):
+def forward_kernel(ang_ref, wave_ref, slow_ref, tw_ref, m_ref, out_ref, zs, total, *, member):
     factor, block = zs.shape[0], zs.shape[1]
     part_width, width = slow_ref.shape[2], out_ref.shape[3]
     scale = ang_ref[member] * depth_step
-
-    def tile(t, carry):
+    step = pl.program_id(0)
+    start = pl.multiple_of(step * block, block)
+    last = pl.num_programs(0) - 1
+
+    @pl.when(step == 0)
+    def _():
+        total[...] = jnp.zeros_like(total)
+
+    def tile(t, sums):
         rows = pl.ds(pl.multiple_of(t * 8, 8), 8)
         cells = []
         for n in range(factor):
             at = n * LANES
             s = slow_ref[at // part_width, rows, pl.ds(at % part_width, LANES)]
+            sums = sums + s
             sn, cs = sin_cos(s * scale)
             re = wave_ref[0, 0, rows, pl.ds(at, LANES)]
             im = wave_ref[1, 0, rows, pl.ds(at, LANES)]
@@ -110,9 +118,9 @@
                 re, im = re * c + im * s, im * c - re * s
             zs[k, rows, pl.ds(0, LANES)] = re
             zs[k, rows, pl.ds(LANES, LANES)] = im
-        return carry
-
-    lax.fori_loop(0, block // 8, tile, 0)
+        return sums
+
+    total[...] = lax.fori_loop(0, block // 8, tile, total[...])
     for g in range(0, factor, 4):
         high, low = split(zs[pl.ds(g, 4)].reshape(4 * block, 2 * LANES))
         y = dot(high, m_ref[0]) + (dot(low, m_ref[0]) + dot(high, m_ref[1]))
@@ -120,13 +128,21 @@
         for j in range(4):
             at = (g + j) * LANES
             cols = pl.ds(at % width, LANES)
-            out_ref[at // width, 0, :, cols] = y[j, :, :LANES]
-            out_ref[at // width, 1, :, cols] = y[j, :, LANES:]
+            out_ref[at // width, 0, pl.ds(start, block), cols] = y[j, :, :LANES]
+            out_ref[at // width, 1, pl.ds(start, block), cols] = y[j, :, LANES:]
+
+    if member == 0:
+        @pl.when(step == last)
+        def _():
+            value = jnp.full((HALO, width), jnp.sum(total[...]), jnp.float32)
+            for d in range(out_ref.shape[0]):
+                for c in range(2):
+                    out_ref[d, c, pl.ds(out_ref.shape[2] - HALO, HALO), :] = value
 
 
 def shift_kernel(ang_ref, mean_ref, in_ref, tw_ref, m_ref, out_ref, zs, *, member):
     factor, width = zs.shape[0], zs.shape[2]
-    strips, rows_in = in_ref.shape[0], in_ref.shape[2]
+    strips, rows_in = in_ref.shape[0], out_ref.shape[2] - HALO
     count = factor * LANES
     base = lax.axis_index("lat") * width
 
@@ -308,15 +324,13 @@
     m_both = jnp.concatenate(
         [split_table(np.ascontiguousarray(right_fwd.T)), split_table(np.ascontiguousarray(right_inv.T))]
     )
-    total = lax.psum(jnp.sum(slowness), ("lat", "freq"))
     copies = jnp.broadcast_to(slowness, (groups,) + slowness.shape)
     strip = lax.all_to_all(copies, "freq", split_axis=0, concat_axis=0, tiled=True)
-    strip, total = lax.optimization_barrier((strip, total))
-    mean_slow = (total / (count_x * full)).reshape(1)
 
     block = 64
 
     def forward(member):
+        tall = rows + HALO if member == 0 else rows
         return pl.pallas_call(
             functools.partial(forward_kernel, member=member),
             grid=(rows // block,),
@@ -327,9 +341,12 @@
                 whole(tw_row),
                 whole(m_fwd),
             ],
-            out_specs=pl.BlockSpec((strips, 2, block, width), lambda i: (0, 0, i, 0)),
-            out_shape=jax.ShapeDtypeStruct((strips, 2, rows, width), jnp.float32),
-            scratch_shapes=[pltpu.VMEM((factor, block, 2 * LANES), jnp.float32)],
+            out_specs=pl.BlockSpec((strips, 2, tall, width), lambda i: (0, 0, 0, 0)),
+            out_shape=jax.ShapeDtypeStruct((strips, 2, tall, width), jnp.float32),
+            scratch_shapes=[
+                pltpu.VMEM((factor, block, 2 * LANES), jnp.float32),
+                pltpu.VMEM((8, LANES), jnp.float32),
+            ],
             compiler_params=params(),
             cost_estimate=pl.CostEstimate(
                 flops=4_000_000_000, bytes_accessed=40_000_000, transcendentals=0
@@ -392,6 +409,8 @@
 
     spectra = [forward(m) for m in range(members)]
     lines = [exchange(s) for s in spectra]
+    total = jnp.sum(lax.slice(lines[0], (0, 0, rows, 0), (strips, 1, rows + 1, 1)))
+    mean_slow = (total / (count_x * full)).reshape(1)
     shifted = [exchange(shift(m, mean_slow, lines[m])) for m in range(members)]
     state = None
     for m in range(members):

time: 522 us -> 491 us (0.941)
  blocking collectives: 87.4 us -> 27.9 us
  waiting for transfers between devices: 312 us -> 337 us
    psum x1 -> x0, blocking collectives: 58.6 us -> none  [local(): total = lax.psum(jnp.sum(slowness), ('lat', 'freq'))]
    all_to_all x1, waiting for transfers between devices: 0.01 us -> 24.9 us  [local(): lax.all_to_all(copies, 'freq', split_axis=0, concat_axis=0, tiled=True)]
  transfers between devices with their start and end apart: 5 -> 5, of which waited for: 4 -> 5; matrix products, arithmetic and copies ran while one was open for 0% -> 0% of each run, Pallas kernels for 12% -> 13%
where the time goes in v3:
time: 491 us; the launch traced here: 490 us
  waiting for transfers between devices  337 us (69%)
  Pallas kernels  90 us (18%)
  blocking collectives  27.9 us (6%)
  starting transfers between devices  24 us (5%)
  local copies, waits for them, and re-layouts  7.25 us (1%)
    all_to_all x4, waiting for transfers between devices, exchange(): return lax.all_to_all(cells, 'lat', split_axis=0, concat_axis=0, tiled=True)  312 us
    pallas_call x2, Pallas kernels, shift(): pl.pallas_call(functools.partial(shift_kernel, member=member), grid=(1,),...  42.3 us
    all_to_all x1, blocking collectives, local(): lax.all_to_all(terms, 'freq', split_axis=0, concat_axis=0, tiled=True)  27.9 us
    pallas_call x2, Pallas kernels, finish(): pl.pallas_call(functools.partial(finish_kernel, member=member, batch_tota...  26.4 us
    all_to_all x1, waiting for transfers between devices, local(): lax.all_to_all(copies, 'freq', split_axis=0, concat_axis=0, tiled=True)  24.9 us
    pallas_call x2, Pallas kernels, forward(): pl.pallas_call(functools.partial(forward_kernel, member=member), grid=(ro...  21.3 us
    all_to_all x4, starting transfers between devices, exchange(): return lax.all_to_all(cells, 'lat', split_axis=0, concat_axis=0, tiled=True)  18.8 us
  transfers between devices with their start and end apart: 5, of which 5 were waited for; matrix products, arithmetic and copies ran while one was open for 0% of the time, Pallas kernels for 13%

profile of v3, /device:TPU:0, one launch (start us, length us, event | category | flops | bytes accessed | tf_op | source)
XLA Modules:
  0.0 489.9 jit_solution(17355645924173933538)
XLA Ops:
  0.6 0.0 copy-start.1
  0.7 2.7 broadcast_in_dim.3
  3.3 5.2 %all-to-all-start = ((f32[4,256,512]{2,1,0:T(8,128)}), f32[4,256,512]{2,1,0:T(8,128)S(1)}, u32[]{:S(2)}, u32[]{:S(2)}) async-start(f32[4,256,512]{2,1,0:T(8,128)} %broadcast_in_dim.3), calls=%async_computation | async-start | bytes 4194304 | tf_op jit(solution)/shard_map/all_to_all | solution.py:328
  8.5 24.9 %all-to-all-done.slow_ref = f32[4,256,512]{2,1,0:T(8,128)S(1)} async-done(((f32[4,256,512]{2,1,0:T(8,128)}), f32[4,256,512]{2,1,0:T(8,128)S(1)}, u32[]{:S(2)}, u32[]{:S(2)}) %all-to-all-start) | async-done | bytes 2097184 | tf_op jit(solution)/shard_map/all_to_all | solution.py:328
  33.4 10.7 %forward.2 = f32[8,2,264,256]{3,2,1,0:T(8,128)} custom-call(f32[2]{0:T(128)S(1)} %convert_multiply_fusion.ang_ref, f32[2,2,256,2048]{3,2,1,0:T(8,128)} %wave_ref.3, f32[4,256,512]{2,1,0:T(8,128)S(1)} %all-to-all-done.slow_ref, f32[2,16,128]{2,1,0:T(8,128)S(1)} %copy-done.1, bf16[2,256,256]{2,1,0:T(8,128)(2,1)S(1)} %copy-done), custom_call_target="tpu_custom_call" | custom-call | flops 4000000000 | bytes 40000000 | tf_op jit(solution)/shard_map/forward/pallas_call | solution.py:334
  44.1 5.0 %all-to-all-start.1 = ((f32[8,2,264,256]{3,2,1,0:T(8,128)}), f32[8,2,264,256]{3,2,1,0:T(8,128)}, u32[]{:S(2)}, u32[]{:S(2)}) async-start(f32[8,2,264,256]{3,2,1,0:T(8,128)} %forward.2), calls=%async_computation.1 | async-start | bytes 8650752 | tf_op jit(solution)/shard_map/all_to_all | solution.py:408
  49.2 10.6 %forward.3 = f32[8,2,256,256]{3,2,1,0:T(8,128)} custom-call(f32[2]{0:T(128)S(1)} %convert_multiply_fusion.ang_ref, f32[2,2,256,2048]{3,2,1,0:T(8,128)} %wave_ref.3, f32[4,256,512]{2,1,0:T(8,128)S(1)} %all-to-all-done.slow_ref, f32[2,16,128]{2,1,0:T(8,128)S(1)} %copy-done.1, bf16[2,256,256]{2,1,0:T(8,128)(2,1)S(1)} %copy-done), custom_call_target="tpu_custom_call" | custom-call | flops 4000000000 | bytes 40000000 | tf_op jit(solution)/shard_map/forward/pallas_call | solution.py:334
  59.7 86.3 %all-to-all-done.1.in_ref = f32[8,2,264,256]{3,2,1,0:T(8,128)} async-done(((f32[8,2,264,256]{3,2,1,0:T(8,128)}), f32[8,2,264,256]{3,2,1,0:T(8,128)}, u32[]{:S(2)}, u32[]{:S(2)}) %all-to-all-start.1) | async-done | bytes 4325408 | tf_op jit(solution)/shard_map/all_to_all | solution.py:408
  146.1 4.6 all-to-all-start.2
  150.7 1.4 slice_reduce_fusion
  152.7 1.6 copy-done.2
  154.3 21.2 %shift.3 = f32[8,2,264,256]{3,2,1,0:T(8,128)} custom-call(f32[2]{0:T(128)S(1)} %convert_multiply_fusion.ang_ref, f32[1]{0:T(128)} %bitcast.mean_ref, f32[8,2,264,256]{3,2,1,0:T(8,128)} %all-to-all-done.1.in_ref, f32[2,16,128,128]{3,2,1,0:T(8,128)S(1)} %copy-done.2, bf16[4,256,256]{2,1,0:T(8,128)(2,1)S(1)} %copy-done.4), custom_call_target="tpu_custom_call" | custom-call | flops 10000000000 | bytes 100000000 | tf_op jit(solution)/shard_map/shift/pallas_call | solution.py:358
  175.5 69.2 %all-to-all-done.2.in_ref = f32[8,2,256,256]{3,2,1,0:T(8,128)} async-done(((f32[8,2,256,256]{3,2,1,0:T(8,128)}), f32[8,2,256,256]{3,2,1,0:T(8,128)}, u32[]{:S(2)}, u32[]{:S(2)}) %all-to-all-start.2) | async-done | bytes 4194336 | tf_op jit(solution)/shard_map/all_to_all | solution.py:408
  244.7 4.6 all-to-all-start.4
  249.3 1.6 copy-done.3
  250.9 21.1 %shift.2 = f32[8,2,264,256]{3,2,1,0:T(8,128)} custom-call(f32[2]{0:T(128)S(1)} %convert_multiply_fusion.ang_ref, f32[1]{0:T(128)} %bitcast.mean_ref, f32[8,2,256,256]{3,2,1,0:T(8,128)} %all-to-all-done.2.in_ref, f32[2,16,128,128]{3,2,1,0:T(8,128)S(1)} %copy-done.3, bf16[4,256,256]{2,1,0:T(8,128)(2,1)S(1)} %copy-done.4), custom_call_target="tpu_custom_call" | custom-call | flops 10000000000 | bytes 100000000 | tf_op jit(solution)/shard_map/shift/pallas_call | solution.py:358
  272.0 74.1 %all-to-all-done.4.in_ref = f32[8,2,264,256]{3,2,1,0:T(8,128)} async-done(((f32[8,2,264,256]{3,2,1,0:T(8,128)}), f32[8,2,264,256]{3,2,1,0:T(8,128)}, u32[]{:S(2)}, u32[]{:S(2)}) %all-to-all-start.4) | async-done | bytes 4325408 | tf_op jit(solution)/shard_map/all_to_all | solution.py:408
  346.1 4.6 all-to-all-start.3
  350.7 13.0 %finish.2 = (f32[2,2,256,2048]{3,2,1,0:T(8,128)}, f32[4,256,512]{2,1,0:T(8,128)S(1)}) custom-call(f32[2]{0:T(128)S(1)} %convert_multiply_fusion.ang_ref, f32[1]{0:T(128)} %bitcast.mean_ref, f32[8,2,264,256]{3,2,1,0:T(8,128)} %all-to-all-done.4.in_ref, f32[2,2,256,2048]{3,2,1,0:T(8,128)} %src_ref.3, f32[4,256,512]{2,1,0:T(8,128)S(1)} %all-to-all-done.slow_ref, ...), custom_call_target="tpu_custom_call" | custom-call | flops 8000000000 | bytes 80000000 | tf_op jit(solution)/shard_map/finish/pallas_call | solution.py:384
  363.7 1.4 copy-done.6
  365.1 82.4 %all-to-all-done.3.in_ref = f32[8,2,264,256]{3,2,1,0:T(8,128)} async-done(((f32[8,2,264,256]{3,2,1,0:T(8,128)}), f32[8,2,264,256]{3,2,1,0:T(8,128)}, u32[]{:S(2)}, u32[]{:S(2)}) %all-to-all-start.3) | async-done | bytes 4325408 | tf_op jit(solution)/shard_map/all_to_all | solution.py:408
  447.5 13.4 %finish.3 = (f32[2,2,256,2048]{3,2,1,0:T(8,128)}, f32[4,256,512]{2,1,0:T(8,128)S(1)}) custom-call(f32[2]{0:T(128)S(1)} %convert_multiply_fusion.ang_ref, f32[1]{0:T(128)} %bitcast.mean_ref, f32[8,2,264,256]{3,2,1,0:T(8,128)} %all-to-all-done.3.in_ref, f32[2,2,256,2048]{3,2,1,0:T(8,128)} %src_ref.3, ...), custom_call_target="tpu_custom_call", output_to_operand_aliasing={{0}: (7, {})} | custom-call | flops 8000000000 | bytes 80000000 | tf_op jit(solution)/shard_map/finish/pallas_call | solution.py:384
  460.9 27.9 %all_to_all.30 = f32[4,256,512]{2,1,0:T(8,128)S(1)} all-to-all(f32[4,256,512]{2,1,0:T(8,128)S(1)} %get-tuple-element.9), channel_id=1, replica_groups=mesh['lat'=8,'freq'=4] {'freq'}, dimensions={0} | all-to-all | bytes 4194304 | tf_op jit(solution)/shard_map/all_to_all | solution.py:420
  488.8 1.0 reduce_sum.19
  (13 shorter events, 0.0 us)
Async XLA Ops:
  0.6 32.7 %copy-start.1 = (f32[2,16,128]{2,1,0:T(8,128)S(1)}, f32[2,16,128]{2,1,0:T(8,128)}, u32[]{:S(2)}) copy-start(f32[2,16,128]{2,1,0:T(8,128)} %constant.19.clone.tw_ref) | copy-start | bytes 49156
  0.6 32.7 %copy-start = (bf16[2,256,256]{2,1,0:T(8,128)(2,1)S(1)}, bf16[2,256,256]{2,1,0:T(8,128)(2,1)}, u32[]{:S(2)}) copy-start(bf16[2,256,256]{2,1,0:T(8,128)(2,1)} %constant.31.m_ref) | copy-start | bytes 786436
  0.7 7.9 %copy-start.7 = (s32[2]{0:T(128)S(1)}, s32[2]{0:T(128)}, u32[]{:S(2)}) copy-start(s32[2]{0:T(128)} %param.17) | copy-start | bytes 28
  3.3 30.0 %all-to-all-start = ((f32[4,256,512]{2,1,0:T(8,128)}), f32[4,256,512]{2,1,0:T(8,128)S(1)}, u32[]{:S(2)}, u32[]{:S(2)}) async-start(f32[4,256,512]{2,1,0:T(8,128)} %broadcast_in_dim.3), calls=%async_computation | async-start | bytes 4194304 | tf_op jit(solution)/shard_map/all_to_all | solution.py:328
  44.1 102.0 %all-to-all-start.1 = ((f32[8,2,264,256]{3,2,1,0:T(8,128)}), f32[8,2,264,256]{3,2,1,0:T(8,128)}, u32[]{:S(2)}, u32[]{:S(2)}) async-start(f32[8,2,264,256]{3,2,1,0:T(8,128)} %forward.2), calls=%async_computation.1 | async-start | bytes 8650752 | tf_op jit(solution)/shard_map/all_to_all | solution.py:408
  59.7 92.9 %copy-start.4 = (bf16[4,256,256]{2,1,0:T(8,128)(2,1)S(1)}, bf16[4,256,256]{2,1,0:T(8,128)(2,1)}, u32[]{:S(2)}) copy-start(bf16[4,256,256]{2,1,0:T(8,128)(2,1)} %constant.35.m_ref) | copy-start | bytes 1572868
  146.1 98.6 %all-to-all-start.2 = ((f32[8,2,256,256]{3,2,1,0:T(8,128)}), f32[8,2,256,256]{3,2,1,0:T(8,128)}, u32[]{:S(2)}, u32[]{:S(2)}) async-start(f32[8,2,256,256]{3,2,1,0:T(8,128)} %forward.3), calls=%async_computation.2 | async-start | bytes 8388608 | tf_op jit(solution)/shard_map/all_to_all | solution.py:408
  152.7 1.6 copy-start.2
  244.7 101.5 %all-to-all-start.4 = ((f32[8,2,264,256]{3,2,1,0:T(8,128)}), f32[8,2,264,256]{3,2,1,0:T(8,128)}, u32[]{:S(2)}, u32[]{:S(2)}) async-start(f32[8,2,264,256]{3,2,1,0:T(8,128)} %shift.3), calls=%async_computation.4 | async-start | bytes 8650752 | tf_op jit(solution)/shard_map/all_to_all | solution.py:408
  249.3 1.6 copy-start.3
  272.0 78.7 %copy-start.5 = (bf16[2,256,256]{2,1,0:T(8,128)(2,1)S(1)}, bf16[2,256,256]{2,1,0:T(8,128)(2,1)}, u32[]{:S(2)}) copy-start(bf16[2,256,256]{2,1,0:T(8,128)(2,1)} %constant.36.m_ref) | copy-start | bytes 786436
  346.1 101.4 %all-to-all-start.3 = ((f32[8,2,264,256]{3,2,1,0:T(8,128)}), f32[8,2,264,256]{3,2,1,0:T(8,128)}, u32[]{:S(2)}, u32[]{:S(2)}) async-start(f32[8,2,264,256]{3,2,1,0:T(8,128)} %shift.2), calls=%async_computation.3 | async-start | bytes 8650752 | tf_op jit(solution)/shard_map/all_to_all | solution.py:408
  363.7 1.4 copy-start.6

commit v4 on v3

--- a/solution.py
+++ b/solution.py
@@ -327,7 +327,7 @@
     copies = jnp.broadcast_to(slowness, (groups,) + slowness.shape)
     strip = lax.all_to_all(copies, "freq", split_axis=0, concat_axis=0, tiled=True)
 
-    block = 64
+    block = 128
 
     def forward(member):
         tall = rows + HALO if member == 0 else rows
@@ -369,7 +369,7 @@
             name="shift",
         )(angular, mean_slow, spectra, tw_x, m_both)
 
-    final_block = 32
+    final_block = 64
 
     def finish(member, mean_slow, lines, before):
         strip_block = pl.BlockSpec((groups, final_block, part_width), lambda i: (0, i, 0))

time: 491 us -> 489 us (level)
  no operation moved by 1% of the time
where the time goes in v4:
time: 489 us; the launch traced here: 488 us
  waiting for transfers between devices  338 us (69%)
  Pallas kernels  86.9 us (18%)
  blocking collectives  27.9 us (6%)
  starting transfers between devices  24 us (5%)
  local copies, waits for them, and re-layouts  7.25 us (1%)
    all_to_all x4, waiting for transfers between devices, exchange(): return lax.all_to_all(cells, 'lat', split_axis=0, concat_axis=0, tiled=True)  314 us
    pallas_call x2, Pallas kernels, shift(): pl.pallas_call(functools.partial(shift_kernel, member=member), grid=(1,),...  42.3 us
    all_to_all x1, blocking collectives, local(): lax.all_to_all(terms, 'freq', split_axis=0, concat_axis=0, tiled=True)  27.9 us
    all_to_all x1, waiting for transfers between devices, local(): lax.all_to_all(copies, 'freq', split_axis=0, concat_axis=0, tiled=True)  24.9 us
    pallas_call x2, Pallas kernels, finish(): pl.pallas_call(functools.partial(finish_kernel, member=member, batch_tota...  23.6 us
    pallas_call x2, Pallas kernels, forward(): pl.pallas_call(functools.partial(forward_kernel, member=member), grid=(ro...  21.1 us
    all_to_all x4, starting transfers between devices, exchange(): return lax.all_to_all(cells, 'lat', split_axis=0, concat_axis=0, tiled=True)  18.8 us
  transfers between devices with their start and end apart: 5, of which 5 were waited for; matrix products, arithmetic and copies ran while one was open for 0% of the time, Pallas kernels for 13%

profile of v4, /device:TPU:0, one launch (start us, length us, event | category | flops | bytes accessed | tf_op | source)
XLA Modules:
  0.0 488.3 jit_solution(702544276225357966)
XLA Ops:
  0.6 0.0 copy-start.1
  0.7 2.7 broadcast_in_dim.3
  3.3 5.2 %all-to-all-start = ((f32[4,256,512]{2,1,0:T(8,128)}), f32[4,256,512]{2,1,0:T(8,128)S(1)}, u32[]{:S(2)}, u32[]{:S(2)}) async-start(f32[4,256,512]{2,1,0:T(8,128)} %broadcast_in_dim.3), calls=%async_computation | async-start | bytes 4194304 | tf_op jit(solution)/shard_map/all_to_all | solution.py:328
  8.5 24.9 %all-to-all-done.slow_ref = f32[4,256,512]{2,1,0:T(8,128)S(1)} async-done(((f32[4,256,512]{2,1,0:T(8,128)}), f32[4,256,512]{2,1,0:T(8,128)S(1)}, u32[]{:S(2)}, u32[]{:S(2)}) %all-to-all-start) | async-done | bytes 2097184 | tf_op jit(solution)/shard_map/all_to_all | solution.py:328
  33.4 10.6 %forward.2 = f32[8,2,264,256]{3,2,1,0:T(8,128)} custom-call(f32[2]{0:T(128)S(1)} %convert_multiply_fusion.ang_ref, f32[2,2,256,2048]{3,2,1,0:T(8,128)} %wave_ref.3, f32[4,256,512]{2,1,0:T(8,128)S(1)} %all-to-all-done.slow_ref, f32[2,16,128]{2,1,0:T(8,128)S(1)} %copy-done.1, bf16[2,256,256]{2,1,0:T(8,128)(2,1)S(1)} %copy-done), custom_call_target="tpu_custom_call" | custom-call | flops 4000000000 | bytes 40000000 | tf_op jit(solution)/shard_map/forward/pallas_call | solution.py:334
  44.0 5.0 %all-to-all-start.1 = ((f32[8,2,264,256]{3,2,1,0:T(8,128)}), f32[8,2,264,256]{3,2,1,0:T(8,128)}, u32[]{:S(2)}, u32[]{:S(2)}) async-start(f32[8,2,264,256]{3,2,1,0:T(8,128)} %forward.2), calls=%async_computation.1 | async-start | bytes 8650752 | tf_op jit(solution)/shard_map/all_to_all | solution.py:408
  49.0 10.5 %forward.3 = f32[8,2,256,256]{3,2,1,0:T(8,128)} custom-call(f32[2]{0:T(128)S(1)} %convert_multiply_fusion.ang_ref, f32[2,2,256,2048]{3,2,1,0:T(8,128)} %wave_ref.3, f32[4,256,512]{2,1,0:T(8,128)S(1)} %all-to-all-done.slow_ref, f32[2,16,128]{2,1,0:T(8,128)S(1)} %copy-done.1, bf16[2,256,256]{2,1,0:T(8,128)(2,1)S(1)} %copy-done), custom_call_target="tpu_custom_call" | custom-call | flops 4000000000 | bytes 40000000 | tf_op jit(solution)/shard_map/forward/pallas_call | solution.py:334
  59.5 86.5 %all-to-all-done.1.in_ref = f32[8,2,264,256]{3,2,1,0:T(8,128)} async-done(((f32[8,2,264,256]{3,2,1,0:T(8,128)}), f32[8,2,264,256]{3,2,1,0:T(8,128)}, u32[]{:S(2)}, u32[]{:S(2)}) %all-to-all-start.1) | async-done | bytes 4325408 | tf_op jit(solution)/shard_map/all_to_all | solution.py:408
  146.0 4.6 all-to-all-start.2
  150.5 1.4 slice_reduce_fusion
  152.6 1.6 copy-done.2
  154.2 21.2 %shift.3 = f32[8,2,264,256]{3,2,1,0:T(8,128)} custom-call(f32[2]{0:T(128)S(1)} %convert_multiply_fusion.ang_ref, f32[1]{0:T(128)} %bitcast.mean_ref, f32[8,2,264,256]{3,2,1,0:T(8,128)} %all-to-all-done.1.in_ref, f32[2,16,128,128]{3,2,1,0:T(8,128)S(1)} %copy-done.2, bf16[4,256,256]{2,1,0:T(8,128)(2,1)S(1)} %copy-done.4), custom_call_target="tpu_custom_call" | custom-call | flops 10000000000 | bytes 100000000 | tf_op jit(solution)/shard_map/shift/pallas_call | solution.py:358
  175.3 69.2 %all-to-all-done.2.in_ref = f32[8,2,256,256]{3,2,1,0:T(8,128)} async-done(((f32[8,2,256,256]{3,2,1,0:T(8,128)}), f32[8,2,256,256]{3,2,1,0:T(8,128)}, u32[]{:S(2)}, u32[]{:S(2)}) %all-to-all-start.2) | async-done | bytes 4194336 | tf_op jit(solution)/shard_map/all_to_all | solution.py:408
  244.5 4.6 all-to-all-start.4
  249.2 1.6 copy-done.3
  250.8 21.1 %shift.2 = f32[8,2,264,256]{3,2,1,0:T(8,128)} custom-call(f32[2]{0:T(128)S(1)} %convert_multiply_fusion.ang_ref, f32[1]{0:T(128)} %bitcast.mean_ref, f32[8,2,256,256]{3,2,1,0:T(8,128)} %all-to-all-done.2.in_ref, f32[2,16,128,128]{3,2,1,0:T(8,128)S(1)} %copy-done.3, bf16[4,256,256]{2,1,0:T(8,128)(2,1)S(1)} %copy-done.4), custom_call_target="tpu_custom_call" | custom-call | flops 10000000000 | bytes 100000000 | tf_op jit(solution)/shard_map/shift/pallas_call | solution.py:358
  271.9 74.1 %all-to-all-done.4.in_ref = f32[8,2,264,256]{3,2,1,0:T(8,128)} async-done(((f32[8,2,264,256]{3,2,1,0:T(8,128)}), f32[8,2,264,256]{3,2,1,0:T(8,128)}, u32[]{:S(2)}, u32[]{:S(2)}) %all-to-all-start.4) | async-done | bytes 4325408 | tf_op jit(solution)/shard_map/all_to_all | solution.py:408
  346.0 4.6 all-to-all-start.3
  350.6 11.6 %finish.2 = (f32[2,2,256,2048]{3,2,1,0:T(8,128)}, f32[4,256,512]{2,1,0:T(8,128)S(1)}) custom-call(f32[2]{0:T(128)S(1)} %convert_multiply_fusion.ang_ref, f32[1]{0:T(128)} %bitcast.mean_ref, f32[8,2,264,256]{3,2,1,0:T(8,128)} %all-to-all-done.4.in_ref, f32[2,2,256,2048]{3,2,1,0:T(8,128)} %src_ref.3, f32[4,256,512]{2,1,0:T(8,128)S(1)} %all-to-all-done.slow_ref, ...), custom_call_target="tpu_custom_call" | custom-call | flops 8000000000 | bytes 80000000 | tf_op jit(solution)/shard_map/finish/pallas_call | solution.py:384
  362.1 1.4 copy-done.6
  363.5 83.9 %all-to-all-done.3.in_ref = f32[8,2,264,256]{3,2,1,0:T(8,128)} async-done(((f32[8,2,264,256]{3,2,1,0:T(8,128)}), f32[8,2,264,256]{3,2,1,0:T(8,128)}, u32[]{:S(2)}, u32[]{:S(2)}) %all-to-all-start.3) | async-done | bytes 4325408 | tf_op jit(solution)/shard_map/all_to_all | solution.py:408
  447.4 12.0 %finish.3 = (f32[2,2,256,2048]{3,2,1,0:T(8,128)}, f32[4,256,512]{2,1,0:T(8,128)S(1)}) custom-call(f32[2]{0:T(128)S(1)} %convert_multiply_fusion.ang_ref, f32[1]{0:T(128)} %bitcast.mean_ref, f32[8,2,264,256]{3,2,1,0:T(8,128)} %all-to-all-done.3.in_ref, f32[2,2,256,2048]{3,2,1,0:T(8,128)} %src_ref.3, ...), custom_call_target="tpu_custom_call", output_to_operand_aliasing={{0}: (7, {})} | custom-call | flops 8000000000 | bytes 80000000 | tf_op jit(solution)/shard_map/finish/pallas_call | solution.py:384
  459.4 27.9 %all_to_all.30 = f32[4,256,512]{2,1,0:T(8,128)S(1)} all-to-all(f32[4,256,512]{2,1,0:T(8,128)S(1)} %get-tuple-element.9), channel_id=1, replica_groups=mesh['lat'=8,'freq'=4] {'freq'}, dimensions={0} | all-to-all | bytes 4194304 | tf_op jit(solution)/shard_map/all_to_all | solution.py:420
  487.3 1.0 reduce_sum.19
  (13 shorter events, 0.0 us)
Async XLA Ops:
  0.6 32.7 %copy-start.1 = (f32[2,16,128]{2,1,0:T(8,128)S(1)}, f32[2,16,128]{2,1,0:T(8,128)}, u32[]{:S(2)}) copy-start(f32[2,16,128]{2,1,0:T(8,128)} %constant.19.clone.tw_ref) | copy-start | bytes 49156
  0.6 32.7 %copy-start = (bf16[2,256,256]{2,1,0:T(8,128)(2,1)S(1)}, bf16[2,256,256]{2,1,0:T(8,128)(2,1)}, u32[]{:S(2)}) copy-start(bf16[2,256,256]{2,1,0:T(8,128)(2,1)} %constant.31.m_ref) | copy-start | bytes 786436
  0.7 7.9 %copy-start.7 = (s32[2]{0:T(128)S(1)}, s32[2]{0:T(128)}, u32[]{:S(2)}) copy-start(s32[2]{0:T(128)} %param.17) | copy-start | bytes 28
  3.3 30.0 %all-to-all-start = ((f32[4,256,512]{2,1,0:T(8,128)}), f32[4,256,512]{2,1,0:T(8,128)S(1)}, u32[]{:S(2)}, u32[]{:S(2)}) async-start(f32[4,256,512]{2,1,0:T(8,128)} %broadcast_in_dim.3), calls=%async_computation | async-start | bytes 4194304 | tf_op jit(solution)/shard_map/all_to_all | solution.py:328
  44.0 101.9 %all-to-all-start.1 = ((f32[8,2,264,256]{3,2,1,0:T(8,128)}), f32[8,2,264,256]{3,2,1,0:T(8,128)}, u32[]{:S(2)}, u32[]{:S(2)}) async-start(f32[8,2,264,256]{3,2,1,0:T(8,128)} %forward.2), calls=%async_computation.1 | async-start | bytes 8650752 | tf_op jit(solution)/shard_map/all_to_all | solution.py:408
  59.5 93.1 %copy-start.4 = (bf16[4,256,256]{2,1,0:T(8,128)(2,1)S(1)}, bf16[4,256,256]{2,1,0:T(8,128)(2,1)}, u32[]{:S(2)}) copy-start(bf16[4,256,256]{2,1,0:T(8,128)(2,1)} %constant.35.m_ref) | copy-start | bytes 1572868
  146.0 98.6 %all-to-all-start.2 = ((f32[8,2,256,256]{3,2,1,0:T(8,128)}), f32[8,2,256,256]{3,2,1,0:T(8,128)}, u32[]{:S(2)}, u32[]{:S(2)}) async-start(f32[8,2,256,256]{3,2,1,0:T(8,128)} %forward.3), calls=%async_computation.2 | async-start | bytes 8388608 | tf_op jit(solution)/shard_map/all_to_all | solution.py:408
  152.6 1.6 copy-start.2
  244.5 101.5 %all-to-all-start.4 = ((f32[8,2,264,256]{3,2,1,0:T(8,128)}), f32[8,2,264,256]{3,2,1,0:T(8,128)}, u32[]{:S(2)}, u32[]{:S(2)}) async-start(f32[8,2,264,256]{3,2,1,0:T(8,128)} %shift.3), calls=%async_computation.4 | async-start | bytes 8650752 | tf_op jit(solution)/shard_map/all_to_all | solution.py:408
  249.2 1.6 copy-start.3
  271.9 78.7 %copy-start.5 = (bf16[2,256,256]{2,1,0:T(8,128)(2,1)S(1)}, bf16[2,256,256]{2,1,0:T(8,128)(2,1)}, u32[]{:S(2)}) copy-start(bf16[2,256,256]{2,1,0:T(8,128)(2,1)} %constant.36.m_ref) | copy-start | bytes 786436
  346.0 101.4 %all-to-all-start.3 = ((f32[8,2,264,256]{3,2,1,0:T(8,128)}), f32[8,2,264,256]{3,2,1,0:T(8,128)}, u32[]{:S(2)}, u32[]{:S(2)}) async-start(f32[8,2,264,256]{3,2,1,0:T(8,128)} %shift.2), calls=%async_computation.3 | async-start | bytes 8650752 | tf_op jit(solution)/shard_map/all_to_all | solution.py:408
  362.1 1.4 copy-start.6
